TPU v7x, 32 devices: a whole 2x2x4 slice. The times are simulated.
32 devices in a mesh: batch: 8 (over z, y), mp: 4 (over x, core).
Axes of the slice: x: 2, y: 2, z: 4, core: 2. Of those that a mesh axis runs over, the one named last changes fastest.
Arguments:
- tokens: bfloat16 [32, 2048, 768], P(('batch', 'mp')), may hold values from -6 to 6
- key_mask: int32 [32, 2048], P(('batch', 'mp')), may hold values 0 or 1
- lengths: int32 [32], P(('batch', 'mp')), may hold values from 1024 to 2048, as said below
- routed: int32 [32, 256], P(('batch', 'mp')), may hold values from 0 to 2047, as said below
- w_router: bfloat16 [768], replicated, may hold values from -0.21875 to 0.21875
- gain_one: bfloat16 [768], replicated, may hold values from 0.25 to 1.75
- gain_two: bfloat16 [768], replicated, may hold values from 0.25 to 1.75
- w_qkv: bfloat16 [768, 2304], replicated, may hold values from -0.21875 to 0.21875
- w_out: bfloat16 [768, 768], replicated, may hold values from -0.625 to 0.625
- w_up: bfloat16 [768, 3072], P(None, 'mp'), may hold values from -0.21875 to 0.21875
- w_down: bfloat16 [3072, 768], P('mp'), may hold values from -0.109375 to 0.109375
- cotangent: bfloat16 [32, 2048, 768], P(('batch', 'mp')), may hold values from -6 to 6
Outputs:
- block_out: bfloat16 [32, 2048, 768], P(('batch', 'mp'))
- grad_tokens: bfloat16 [32, 2048, 768], P(('batch', 'mp'))
- grad_router: float32 [768], P('batch')
- grad_gain_one: float32 [768], P('batch')
- grad_gain_two: float32 [768], P('batch')
- grad_qkv: float32 [768, 2304], P('batch')
- grad_out: float32 [768, 768], P('batch')
- grad_up: float32 [768, 3072], P('batch', 'mp')
- grad_down: float32 [3072, 768], P('mp', 'batch')
Inputs may be any that keep to these rules, and one draw needn't show every extreme that they name: Each length is a multiple of 8. For every sequence s with s // 4 even, lengths[s] + lengths[s + 4] = 3072. One sequence, drawn from the seed, has 2048 and its partner 2048 // 2. `routed`: row s holds in its first lengths[s] // 8 entries distinct positions below lengths[s] in rising order, the last of them lengths[s] - 1; its other entries are 0.
All inputs are finite; a program needn't handle non-finite values. No bound on the sum of `key_mask` on one device may be relied on, other than what follows from the above.
Results may differ from a plain program's by a relative error of at most 0.015.
Values may be sent and summed in bfloat16 or wider, within the bound.
A program may use at most 192 MiB of HBM per device.

v0:
```python
import jax
import jax.numpy as jnp
from jax import lax
from jax.sharding import PartitionSpec as P

HEADS = 12


EPSILON = 1e-06


def split_up(x, dim, peers):
    before, after = (x.shape[:dim], x.shape[dim + 1 :])
    return jnp.moveaxis(x.reshape(*before, peers, -1, *after), dim, 0)


def sum_at_owner(x, axis, dim):
    blocks = split_up(x, dim, lax.axis_size(axis))
    arrived = lax.all_to_all(blocks, axis, split_axis=0, concat_axis=0, tiled=True)
    return arrived.astype(jnp.float32).sum(axis=0)


def rms_scale(v, g):
    return v * lax.rsqrt(jnp.mean(v * v, axis=-1, keepdims=True) + EPSILON) * g


def masked_probs(scores, allowed):
    shifted = jnp.where(allowed, scores, -1e30)
    shifted = shifted - jnp.max(shifted, axis=-1, keepdims=True)
    exp_scores = jnp.exp(shifted)
    return exp_scores / jnp.sum(exp_scores, axis=-1, keepdims=True)


def local(
    tokens,
    key_mask,
    lengths,
    routed,
    w_router,
    gain_one,
    gain_two,
    w_qkv,
    w_out,
    w_up,
    w_down,
    cotangent,
):
    model_width = tokens.shape[2]
    head_count = HEADS
    head_size = model_width // head_count
    routed_max = routed.shape[1]
    batch_size = lax.axis_size("batch")
    slot_cap = -(-routed_max // batch_size)
    padded_rows = slot_cap * batch_size
    score_scale = head_size ** (-0.5)
    seq_tokens = tokens[0]
    live_count = lengths[0] // 8
    select_ids = routed[0]
    slot_ids = jnp.arange(padded_rows, dtype=jnp.int32)
    live_mask = (slot_ids < live_count).astype(jnp.float32)
    picked = jnp.take(seq_tokens, select_ids, axis=0)
    float_rows = picked.astype(jnp.float32)
    gate_logit = jnp.dot(picked, w_router, preferred_element_type=jnp.float32)
    gate_rate, sigmoid_back = jax.vjp(jax.nn.sigmoid, gate_logit)
    normed_one, norm_one_back = jax.vjp(rms_scale, float_rows, gain_one.astype(jnp.float32))
    first_low = normed_one.astype(jnp.bfloat16)
    qkv_rows = jnp.dot(first_low, w_qkv, preferred_element_type=jnp.float32).astype(jnp.bfloat16)
    queries = qkv_rows[:, :model_width].reshape(padded_rows, head_count, head_size)
    key_heads = qkv_rows[:, model_width : 2 * model_width].reshape(
        padded_rows, head_count, head_size
    )
    values = qkv_rows[:, 2 * model_width :].reshape(padded_rows, head_count, head_size)
    scores = (
        jnp.einsum("qhd,khd->hqk", queries, key_heads, preferred_element_type=jnp.float32)
        * score_scale
    )
    key_open = jnp.take(key_mask[0], select_ids) == 1
    allowed = (slot_ids[None, :] < slot_ids[:, None]) & key_open[None, :] | (
        slot_ids[None, :] == slot_ids[:, None]
    )
    attn_probs, probs_back = jax.vjp(lambda table: masked_probs(table, allowed[None]), scores)
    probs_low = attn_probs.astype(jnp.bfloat16)
    mixed = jnp.einsum("hqk,khd->qhd", probs_low, values, preferred_element_type=jnp.float32)
    mixed = mixed.reshape(padded_rows, model_width).astype(jnp.bfloat16)
    attended = jnp.dot(mixed, w_out, preferred_element_type=jnp.float32)
    residual = float_rows + attended
    normed_two, norm_two_back = jax.vjp(rms_scale, residual, gain_two.astype(jnp.float32))
    second_low = normed_two.astype(jnp.bfloat16)
    gathered = lax.all_gather(second_low, "mp", axis=0, tiled=True)
    pre_act = jnp.dot(gathered, w_up, preferred_element_type=jnp.float32)
    activation = jax.nn.gelu(pre_act).astype(jnp.bfloat16)
    mlp_low = lax.psum_scatter(
        jnp.dot(activation, w_down, preferred_element_type=jnp.float32).astype(jnp.bfloat16),
        "mp",
        scatter_dimension=0,
        tiled=True,
    )
    branch = attended + mlp_low.astype(jnp.float32)
    route_gain = live_mask * gate_rate
    block_out = (
        seq_tokens.astype(jnp.float32)
        .at[select_ids]
        .add(route_gain[:, None] * branch)
        .astype(jnp.bfloat16)
    )
    cot_rows = jnp.take(cotangent[0], select_ids, axis=0).astype(jnp.float32)
    grad_rate = live_mask * jnp.sum(cot_rows * branch, axis=-1)
    grad_logit = sigmoid_back(grad_rate)[0]
    grad_branch = route_gain[:, None] * cot_rows
    grad_mlp = grad_branch.astype(jnp.bfloat16)
    regathered, grad_gathered = (
        lax.all_gather(second_low, "mp", axis=0, tiled=True),
        lax.all_gather(grad_mlp, "mp", axis=0, tiled=True),
    )
    pre_again = jnp.dot(regathered, w_up, preferred_element_type=jnp.float32)
    act_again = jax.nn.gelu(pre_again).astype(jnp.bfloat16)
    grad_act = jnp.dot(grad_gathered, w_down.T, preferred_element_type=jnp.float32)
    _, gelu_back = jax.vjp(jax.nn.gelu, pre_again)
    grad_pre = gelu_back(grad_act)[0].astype(jnp.bfloat16)
    grad_down_local = jnp.dot(act_again.T, grad_gathered, preferred_element_type=jnp.float32)
    grad_up_local = jnp.dot(regathered.T, grad_pre, preferred_element_type=jnp.float32)
    grad_second = lax.psum_scatter(
        jnp.dot(grad_pre, w_up.T, preferred_element_type=jnp.float32),
        "mp",
        scatter_dimension=0,
        tiled=True,
    ).astype(jnp.bfloat16)
    grad_residual, grad_gain_two_local = norm_two_back(grad_second.astype(jnp.float32))
    grad_attended = (grad_branch + grad_residual).astype(jnp.bfloat16)
    grad_out_local = jnp.dot(mixed.T, grad_attended, preferred_element_type=jnp.float32)
    grad_mixed = jnp.dot(grad_attended, w_out.T, preferred_element_type=jnp.float32).astype(
        jnp.bfloat16
    )
    grad_mixed = grad_mixed.reshape(padded_rows, head_count, head_size)
    grad_probs = jnp.einsum("qhd,khd->hqk", grad_mixed, values, preferred_element_type=jnp.float32)
    grad_scores = probs_back(grad_probs)[0].astype(jnp.bfloat16)
    grad_queries = (
        jnp.einsum("hqk,khd->qhd", grad_scores, key_heads, preferred_element_type=jnp.float32)
        * score_scale
    )
    grad_keys = (
        jnp.einsum("hqk,qhd->khd", grad_scores, queries, preferred_element_type=jnp.float32)
        * score_scale
    )
    grad_values = jnp.einsum(
        "hqk,qhd->khd", probs_low, grad_mixed, preferred_element_type=jnp.float32
    )
    grad_qkv_rows = jnp.concatenate(
        [
            grad_queries.reshape(padded_rows, model_width),
            grad_keys.reshape(padded_rows, model_width),
            grad_values.reshape(padded_rows, model_width),
        ],
        axis=1,
    ).astype(jnp.bfloat16)
    grad_qkv_local = jnp.dot(first_low.T, grad_qkv_rows, preferred_element_type=jnp.float32)
    grad_first = jnp.dot(grad_qkv_rows, w_qkv.T, preferred_element_type=jnp.float32)
    grad_norm_rows, grad_gain_one_local = norm_one_back(grad_first)
    grad_picked = (
        grad_norm_rows + grad_residual + grad_logit[:, None] * w_router.astype(jnp.float32)[None, :]
    )
    grad_router_local = jnp.sum(grad_logit[:, None] * float_rows, axis=0)
    grad_tokens = (
        cotangent[0].astype(jnp.float32).at[select_ids].add(live_mask[:, None] * grad_picked)
    )
    grad_tokens = grad_tokens.astype(jnp.bfloat16)
    grad_up, grad_down = (
        sum_at_owner(grad_up_local.astype(jnp.bfloat16), "batch", 0),
        sum_at_owner(grad_down_local.astype(jnp.bfloat16), "batch", 1),
    )
    qkv_share, out_share, one_share, two_share, router_share = (
        lax.psum_scatter(grad_qkv_local, "batch", scatter_dimension=0, tiled=True),
        lax.psum_scatter(grad_out_local, "batch", scatter_dimension=0, tiled=True),
        lax.psum_scatter(grad_gain_one_local, "batch", scatter_dimension=0, tiled=True),
        lax.psum_scatter(grad_gain_two_local, "batch", scatter_dimension=0, tiled=True),
        lax.psum_scatter(grad_router_local, "batch", scatter_dimension=0, tiled=True),
    )
    grad_qkv, grad_out, grad_gain_one, grad_gain_two, grad_router = (
        lax.psum(qkv_share.astype(jnp.bfloat16), "mp").astype(jnp.float32),
        lax.psum(out_share.astype(jnp.bfloat16), "mp").astype(jnp.float32),
        lax.psum(one_share.astype(jnp.bfloat16), "mp").astype(jnp.float32),
        lax.psum(two_share.astype(jnp.bfloat16), "mp").astype(jnp.float32),
        lax.psum(router_share.astype(jnp.bfloat16), "mp").astype(jnp.float32),
    )
    return (
        block_out[None],
        grad_tokens[None],
        grad_router,
        grad_gain_one,
        grad_gain_two,
        grad_qkv,
        grad_out,
        grad_up,
        grad_down,
    )


def solution(mesh):
    in_specs = (
        P(("batch", "mp"), None, None),
        P(("batch", "mp"), None),
        P(("batch", "mp")),
        P(("batch", "mp"), None),
        P(),
        P(),
        P(),
        P(),
        P(),
        P(None, "mp"),
        P("mp", None),
        P(("batch", "mp"), None, None),
    )
    out_specs = (
        P(("batch", "mp"), None, None),
        P(("batch", "mp"), None, None),
        P("batch"),
        P("batch"),
        P("batch"),
        P("batch", None),
        P("batch", None),
        P("batch", "mp"),
        P("mp", "batch"),
    )
    return jax.shard_map(local, mesh=mesh, in_specs=in_specs, out_specs=out_specs, check_vma=False)
```

profile of v0, /device:TPU:0, one launch (start us, length us, event | category | flops | bytes accessed | tf_op | source)
XLA Modules:
  0.0 474.1 jit_solution(8771090763176671056)
XLA Ops:
  13.4 2.5 gather_fusion
  17.3 4.5 gather_fusion.1
  23.1 1.9 fusion.57
  25.0 4.5 gather_fusion.2
  29.5 2.1 convolution_convert_fusion
  32.7 1.9 copy.43
  34.6 1.9 copy.42
  36.5 1.9 copy.41
  38.4 1.8 fusion.8
  42.5 3.3 convert_reduce_fusion
  46.5 1.9 convolution_convert_fusion.6
  49.3 3.6 fusion.12
  54.9 2.3 multiply_convert_fusion.1
  57.5 18.0 %all-gather.5.cloned.1.call-done = bf16[1024,768]{1,0:T(8,128)(2,1)} async-done(((bf16[256,768]{1,0:T(8,128)(2,1)}), bf16[1024,768]{1,0:T(8,128)(2,1)}) %all-gather.5.cloned.1.call-update) | async-done | bytes 1572880 | tf_op jit(solution)/shard_map/all_gather | solution.py:113
  75.4 4.8 %fusion.61 = f32[1024,768]{1,0:T(8,128)} fusion(bf16[1024,768]{1,0:T(8,128)(2,1)} %all-gather.5.cloned.1.call-done, bf16[768,768]{1,0:T(8,128)(2,1)} %param.24), kind=kOutput, calls=%fused_computation.127 | convolution fusion | flops 1207959552 | bytes 5898240 | tf_op jit(solution)/shard_map/dot_general | solution.py:117
  80.2 16.4 %all-gather.3.cloned.1.call-done = bf16[1024,768]{1,0:T(8,128)(2,1)} async-done(((bf16[256,768]{1,0:T(8,128)(2,1)}), bf16[1024,768]{1,0:T(8,128)(2,1)}) %all-gather.3.cloned.1.call-update) | async-done | bytes 1572880 | tf_op jit(solution)/shard_map/all_gather | solution.py:89
  96.7 6.9 %fusion.6 = (bf16[1024,768]{1,0:T(8,128)(2,1)}, f32[1024,768]{1,0:T(8,128)S(1)}) fusion(f32[1024,768]{1,0:T(8,128)} %fusion.61, bf16[1024,768]{1,0:T(8,128)(2,1)} %all-gather.3.cloned.1.call-done, bf16[768,768]{1,0:T(8,128)(2,1)} %param.23), kind=kOutput, calls=%fused_computation.14 | convolution fusion | flops 1223688192 | bytes 10616832 | tf_op jit(solution)/shard_map/dot_general | solution.py:90
  103.6 1.7 copy-done.60
  105.3 3.2 convolution_convert_fusion.1
  108.5 4.8 %fusion.62 = f32[1024,768]{1,0:T(8,128)} fusion(bf16[1024,768]{1,0:T(8,128)(2,1)} %get-tuple-element.38, bf16[768,768]{1,0:T(8,128)(2,1)} %param.23), kind=kOutput, calls=%fused_computation.128 | convolution fusion | flops 1207959552 | bytes 5898240 | tf_op jit(solution)/shard_map/dot_general | solution.py:123
  113.4 23.4 %reduce-scatter.5.cloned.1.call-done = bf16[256,768]{1,0:T(8,128)(2,1)} async-done(((bf16[1024,768]{1,0:T(8,128)(2,1)}), bf16[256,768]{1,0:T(8,128)(2,1)}) %reduce-scatter.5.cloned.1.call-update) | async-done | bytes 393232 | tf_op jit(solution)/shard_map/reduce_scatter | solution.py:92
  136.8 41.1 %reduce-scatter.7.cloned.1.call-done = f32[256,768]{1,0:T(8,128)} async-done(((f32[1024,768]{1,0:T(8,128)}), f32[256,768]{1,0:T(8,128)}) %reduce-scatter.7.cloned.1.call-update) | async-done | bytes 786448 | tf_op jit(solution)/shard_map/reduce_scatter | solution.py:122
  178.0 3.0 fusion.23
  182.5 1.9 fusion.63
  186.0 2.7 convolution_convert_fusion.5
  188.7 2.0 copy.45
  190.6 3.6 multiply_reduce_fusion
  198.8 4.2 fusion.37
  202.9 5.1 %convolution_convert_fusion.2 = bf16[768,768]{0,1:T(8,128)(2,1)} fusion(bf16[1024,768]{1,0:T(8,128)(2,1)} %all-gather.5.cloned.1.call-done, f32[1024,768]{1,0:T(8,128)} %copy-done.60), kind=kOutput, calls=%fused_computation.36 | convolution fusion | flops 1215627264 | bytes 5898240 | tf_op jit(solution)/shard_map/dot_general | solution.py:120
  208.1 5.7 %all-to-all-start.1 = ((bf16[8,768,96]{1,2,0:T(8,128)(2,1)}), bf16[8,768,96]{1,2,0:T(8,128)(2,1)}, u32[]{:S(2)}, u32[]{:S(2)}) async-start(bf16[8,768,96]{1,2,0:T(8,128)(2,1)} %bitcast.90), calls=%async_computation.5 | async-start | bytes 2359296 | tf_op jit(solution)/shard_map/all_to_all | solution.py:19
  213.7 4.4 convolution_convert_fusion.3
  218.1 24.7 %all-to-all-done.1 = bf16[8,768,96]{1,2,0:T(8,128)(2,1)} async-done(((bf16[8,768,96]{1,2,0:T(8,128)(2,1)}), bf16[8,768,96]{1,2,0:T(8,128)(2,1)}, u32[]{:S(2)}, u32[]{:S(2)}) %all-to-all-start.1) | async-done | bytes 1179680 | tf_op jit(solution)/shard_map/all_to_all | solution.py:19
  242.8 4.3 all-to-all-start
  249.8 5.3 %bitcast_convert_fusion.1 = f32[2048,768]{1,0:T(8,128)} fusion(bf16[1,2048,768]{2,1,0:T(8,128)(2,1)} %param.14), kind=kLoop, calls=%fused_computation.123 | loop fusion | flops 1572864 | bytes 9437184 | tf_op jit(solution)/shard_map/convert_element_type | solution.py:101
  255.1 3.2 bitcast_convert_fusion
  258.3 2.2 convert_reduce_fusion.1
  260.4 24.5 %all-to-all-done = bf16[8,96,768]{2,1,0:T(8,128)(2,1)} async-done(((bf16[8,96,768]{2,1,0:T(8,128)(2,1)}), bf16[8,96,768]{2,1,0:T(8,128)(2,1)}, u32[]{:S(2)}, u32[]{:S(2)}) %all-to-all-start) | async-done | bytes 1179680 | tf_op jit(solution)/shard_map/all_to_all | solution.py:19
  284.9 2.2 convert_reduce_fusion.2
  287.1 8.9 %scatter_custom_fusion = f32[2048,768]{1,0:T(8,128)} fusion(f32[2048,768]{1,0:T(8,128)} %bitcast_convert_fusion.1, s32[256]{0:T(256)} %bitcast.94, f32[256,768]{1,0:T(8,128)} %get-tuple-element.37, bf16[256,768]{1,0:T(8,128)(2,1)} %reduce-scatter.5.cloned.1.call-done, f32[256]{0:T(256)S(1)} %copy-done.49), kind=kCustom, calls=%fused_computation.74 | custom fusion | flops 786432 | bytes 7472128 | tf_op jit(solution)/shard_map/scatter-add | solution.py:103
  296.1 4.9 %convert_bitcast_fusion.1 = bf16[1,2048,768]{2,1,0:T(8,128)(2,1)} fusion(f32[2048,768]{1,0:T(8,128)} %scatter_custom_fusion), kind=kLoop, calls=%fused_computation.20 | loop fusion | flops 1572864 | bytes 9437184 | tf_op jit(solution)/shard_map/broadcast_in_dim | solution.py:186
  301.1 2.8 fusion.19
  304.5 9.4 %scatter_custom_fusion.1 = f32[2048,768]{1,0:T(8,128)} fusion(f32[2048,768]{1,0:T(8,128)} %bitcast_convert_fusion, s32[256]{0:T(256)} %bitcast.95, f32[256,768]{1,0:T(8,128)} %get-tuple-element.42, f32[768]{0:T(1024)} %convert_element_type.158, f32[256]{0:T(256)} %copy-done.52, f32[256]{0:T(256)} %multiply_multiply_fusion.2, f32[256]{0:T(256)} %fusion.51, ...), kind=kCustom, calls=%fused_computation.68 | custom fusion | flops 3735552 | bytes 8667392 | tf_op jit(solution)/shard_map/scatter-add | solution.py:164
  315.5 95.6 %reduce-scatter.9.cloned.1.call-done = f32[96,2304]{1,0:T(8,128)} async-done(((f32[768,2304]{1,0:T(8,128)}), f32[96,2304]{1,0:T(8,128)}) %reduce-scatter.9.cloned.1.call-update) | async-done | bytes 884752 | tf_op jit(solution)/shard_map/reduce_scatter | solution.py:172
  411.1 2.0 convert_element_type.166
  413.1 4.8 %convert_bitcast_fusion = bf16[1,2048,768]{2,1,0:T(8,128)(2,1)} fusion(f32[2048,768]{1,0:T(8,128)} %scatter_custom_fusion.1), kind=kLoop, calls=%fused_computation.15 | loop fusion | flops 1572864 | bytes 9437184 | tf_op jit(solution)/shard_map/broadcast_in_dim | solution.py:187
  417.9 35.2 %all-reduce.3 = (bf16[768]{0:T(1024)(128)(2,1)}, bf16[768]{0:T(1024)(128)(2,1)}, bf16[768]{0:T(1024)(128)(2,1)S(1)}) all-reduce(f32[768]{0:T(1024)S(1)} %copy-done.54, f32[768]{0:T(1024)S(1)} %copy-done.53, f32[768]{0:T(1024)S(1)} %copy-done.43), channel_id=4, replica_groups=mesh['batch'=8,'mp'=4] {'batch'}, use_global_device_ids=true, to_apply=%region_15.17.clone | all-reduce | flops 2304 | bytes 13824
  455.2 6.3 %all-reduce.4 = (bf16[96]{0:T(256)(128)(2,1)}, bf16[96]{0:T(256)(128)(2,1)S(1)}, bf16[96]{0:T(256)(128)(2,1)S(1)}) all-reduce(bf16[96]{0:T(256)(128)(2,1)S(1)} %dynamic-slice.11, bf16[96]{0:T(256)(128)(2,1)S(1)} %dynamic-slice.10, bf16[96]{0:T(256)(128)(2,1)} %dynamic-slice.9), channel_id=1, replica_groups=mesh['batch'=8,'mp'=4] {'mp'}, use_global_device_ids=true, to_apply=%region_16.18 | all-reduce | flops 288 | bytes 1152 | tf_op jit(solution)/shard_map/psum | solution.py:183
  465.3 2.0 convert_element_type.167
  (175 shorter events, 33.0 us)
Async XLA Ops:
  7.2 22.3 %copy-start = (bf16[768,2304]{1,0:T(8,128)(2,1)S(1)}, bf16[768,2304]{1,0:T(8,128)(2,1)}, u32[]{:S(2)}) copy-start(bf16[768,2304]{1,0:T(8,128)(2,1)} %param.21) | copy-start | bytes 10616836
  7.2 68.2 %all-gather.5.cloned.1.call-start = ((), (), s32[]{:S(2)}) async-start(), calls=%async_computation.8 | async-start | bytes 1966080 | tf_op jit(solution)/shard_map/all_gather | solution.py:113
  8.1 21.4 %copy-start.37 = (pred[256]{0:T(512)(128)(4,1)}, pred[256]{0:T(512)(128)(4,1)S(1)}, u32[]{:S(2)}) copy-start(pred[256]{0:T(512)(128)(4,1)S(1)} %compare_and_fusion) | copy-start | bytes 772
  12.8 16.7 %copy-start.28 = (f32[768]{0:T(1024)}, f32[768]{0:T(1024)S(1)}, u32[]{:S(2)}) copy-start(f32[768]{0:T(1024)S(1)} %convert_element_type.134) | copy-start | bytes 9220
  15.9 7.2 %copy-start.57 = (bf16[768,1]{0,1:T(2,128)(2,1)S(1)}, bf16[768,1]{0,1:T(2,128)(2,1)}, u32[]{:S(2)}) copy-start(bf16[768,1]{0,1:T(2,128)(2,1)} %reshape.251) | copy-start | bytes 4612
  25.0 6.7 %copy-start.40 = (f32[256]{0:T(256)}, f32[256]{0:T(256)S(1)}, u32[]{:S(2)}) copy-start(f32[256]{0:T(256)S(1)} %fusion.53) | copy-start | bytes 3076
  46.5 6.3 %copy-start.47 = (f32[256]{0:T(256)}, f32[256]{0:T(256)S(1)}, u32[]{:S(2)}) copy-start(f32[256]{0:T(256)S(1)} %fusion.52) | copy-start | bytes 3076
  52.9 43.8 %all-gather.3.cloned.1.call-start = ((), (), s32[]{:S(2)}) async-start(), calls=%async_computation.6 | async-start | bytes 1966080 | tf_op jit(solution)/shard_map/all_gather | solution.py:89
  57.2 79.5 %reduce-scatter.5.cloned.1.call-start = ((), (), s32[]{:S(2)}) async-start(), calls=%async_computation.7 | async-start | bytes 1966080 | tf_op jit(solution)/shard_map/reduce_scatter | solution.py:92
  96.7 8.6 %copy-start.58 = (bf16[768,768]{1,0:T(8,128)(2,1)S(1)}, bf16[768,768]{1,0:T(8,128)(2,1)}, u32[]{:S(2)}) copy-start(bf16[768,768]{1,0:T(8,128)(2,1)} %param.24) | copy-start | bytes 3538948
  108.5 69.4 %reduce-scatter.7.cloned.1.call-start = ((), (), s32[]{:S(2)}) async-start(), calls=%async_computation.9 | async-start | bytes 3932160 | tf_op jit(solution)/shard_map/reduce_scatter | solution.py:122
  113.4 200.5 %reduce-scatter.11.cloned.1.call-start = ((), (), s32[]{:S(2)}) async-start(), calls=%async_computation.11 | async-start | bytes 2654208 | tf_op jit(solution)/shard_map/reduce_scatter | solution.py:173
  177.9 3.1 copy-start.56
  177.9 3.1 copy-start.3
  177.9 3.1 copy-start.4
  177.9 3.1 copy-start.17
  177.9 3.1 copy-start.31
  177.9 3.1 copy-start.35
  177.9 3.1 copy-start.38
  177.9 3.1 copy-start.48
  177.9 4.6 copy-start.25
  184.4 226.7 %reduce-scatter.9.cloned.1.call-start = ((), (), s32[]{:S(2)}) async-start(), calls=%async_computation.10 | async-start | bytes 7962624 | tf_op jit(solution)/shard_map/reduce_scatter | solution.py:172
  190.6 3.6 copy-start.2
  190.6 3.7 copy-start.11
  190.6 3.7 copy-start.27
  194.3 2.1 copy-start.9
  194.4 2.1 copy-start.16
  208.1 34.8 %all-to-all-start.1 = ((bf16[8,768,96]{1,2,0:T(8,128)(2,1)}), bf16[8,768,96]{1,2,0:T(8,128)(2,1)}, u32[]{:S(2)}, u32[]{:S(2)}) async-start(bf16[8,768,96]{1,2,0:T(8,128)(2,1)} %bitcast.90), calls=%async_computation.5 | async-start | bytes 2359296 | tf_op jit(solution)/shard_map/all_to_all | solution.py:19
  213.7 33.7 %copy-start.50 = (bf16[768]{0:T(1024)(128)(2,1)S(1)}, bf16[768]{0:T(1024)(128)(2,1)}, u32[]{:S(2)}) copy-start(bf16[768]{0:T(1024)(128)(2,1)} %param.18) | copy-start | bytes 4612
  213.7 34.3 %copy-start.59 = (u32[32]{0:T(128)S(1)}, u32[32]{0:T(128)}, u32[]{:S(2)}) copy-start(u32[32]{0:T(128)} %constant.89) | copy-start | bytes 388
  242.8 42.1 %all-to-all-start = ((bf16[8,96,768]{2,1,0:T(8,128)(2,1)}), bf16[8,96,768]{2,1,0:T(8,128)(2,1)}, u32[]{:S(2)}, u32[]{:S(2)}) async-start(bf16[8,96,768]{2,1,0:T(8,128)(2,1)} %bitcast.89), calls=%async_computation.4 | async-start | bytes 2359296 | tf_op jit(solution)/shard_map/all_to_all | solution.py:19
  247.1 216.5 %all-reduce.8.cloned.1.call-start = ((), (), s32[]{:S(2)}) async-start(), calls=%async_computation.12 | async-start | bytes 1179648 | tf_op jit(solution)/shard_map/psum | solution.py:179
  249.8 5.3 %copy-start.8 = (bf16[1,2048,768]{2,1,0:T(8,128)(2,1)S(1)}, bf16[1,2048,768]{2,1,0:T(8,128)(2,1)}, u32[]{:S(2)}) copy-start(bf16[1,2048,768]{2,1,0:T(8,128)(2,1)} %param.25) | copy-start | bytes 9437188
  255.1 32.0 %copy-start.49 = (f32[256]{0:T(256)S(1)}, f32[256]{0:T(256)}, u32[]{:S(2)}) copy-start(f32[256]{0:T(256)} %copy-done.47) | copy-start | bytes 3076
  296.1 4.9 %copy-start.51 = (f32[256]{0:T(256)S(1)}, f32[256]{0:T(256)}, u32[]{:S(2)}) copy-start(f32[256]{0:T(256)} %get-tuple-element.14) | copy-start | bytes 3076
  296.1 4.9 %copy-start.55 = (f32[1,256]{1,0:T(1,128)S(1)}, f32[1,256]{1,0:T(1,128)}, u32[]{:S(2)}) copy-start(f32[1,256]{1,0:T(1,128)} %fusion.57) | copy-start | bytes 3076
  296.1 4.9 %copy-start.6 = (bf16[256,768]{1,0:T(8,128)(2,1)S(1)}, bf16[256,768]{1,0:T(8,128)(2,1)}, u32[]{:S(2)}) copy-start(bf16[256,768]{1,0:T(8,128)(2,1)} %gather_fusion.1) | copy-start | bytes 1179652
  296.1 5.0 %copy-start.19 = (bf16[12,64,256]{2,1,0:T(8,128)(2,1)S(1)}, bf16[12,64,256]{2,1,0:T(8,128)(2,1)}, u32[]{:S(2)}) copy-start(bf16[12,64,256]{2,1,0:T(8,128)(2,1)} %copy-done.18) | copy-start | bytes 1179652
  296.1 5.0 %copy-start.21 = (bf16[12,64,256]{2,1,0:T(8,128)(2,1)S(1)}, bf16[12,64,256]{2,1,0:T(8,128)(2,1)}, u32[]{:S(2)}) copy-start(bf16[12,64,256]{2,1,0:T(8,128)(2,1)} %copy-done.20) | copy-start | bytes 1179652
  296.1 5.0 %copy-start.23 = (bf16[12,64,256]{2,1,0:T(8,128)(2,1)S(1)}, bf16[12,64,256]{2,1,0:T(8,128)(2,1)}, u32[]{:S(2)}) copy-start(bf16[12,64,256]{2,1,0:T(8,128)(2,1)} %copy-done.22) | copy-start | bytes 1179652
  296.1 5.0 %copy-start.42 = (f32[256]{0:T(256)S(1)}, f32[256]{0:T(256)}, u32[]{:S(2)}) copy-start(f32[256]{0:T(256)} %copy-done.40) | copy-start | bytes 3076
  301.1 2.8 copy-start.52
  301.1 2.8 copy-start.46
  301.1 3.4 copy-start.32
  301.1 3.4 copy-start.36
  413.1 4.8 %copy-start.43 = (f32[768]{0:T(1024)S(1)}, f32[768]{0:T(1024)}, u32[]{:S(2)}) copy-start(f32[768]{0:T(1024)} %get-tuple-element.10) | copy-start | bytes 9220
  413.1 4.8 %copy-start.53 = (f32[768]{0:T(1024)S(1)}, f32[768]{0:T(1024)}, u32[]{:S(2)}) copy-start(f32[768]{0:T(1024)} %get-tuple-element.12) | copy-start | bytes 9220
  413.1 4.8 %copy-start.54 = (f32[768]{0:T(1024)S(1)}, f32[768]{0:T(1024)}, u32[]{:S(2)}) copy-start(f32[768]{0:T(1024)} %get-tuple-element.15) | copy-start | bytes 9220
  (22 other events, 26.7 us)
Sparse Core Ops, SparseCore 0:
  53.0 22.3 all-gather.4
  77.0 19.6 all-gather.2
  108.6 28.1 reduce-scatter.4
  139.9 37.9 reduce-scatter.6
  184.5 96.7 reduce-scatter.10
  284.9 126.1 reduce-scatter.8
  414.3 32.6 all-reduce.7
where the time goes:
time: 476 us; the launch traced here: 474 us
  waiting for transfers between devices  244 us (51%)
  other arithmetic  72.9 us (15%)
  matrix products  57.8 us (12%)
  blocking collectives  41.5 us (9%)
  local copies, waits for them, and re-layouts  31.2 us (7%)
  between operations  16.1 us (3%)
  starting transfers between devices  10.9 us (2%)
    reduce_scatter x1, waiting for transfers between devices, local(): lax.psum_scatter(grad_qkv_local, 'batch', scatter_dimension=0, tiled=True)  95.6 us
    all_to_all x2, waiting for transfers between devices, sum_at_owner(): lax.all_to_all(blocks, axis, split_axis=0, concat_axis=0, tiled=True)  49.2 us
    reduce_scatter x1, waiting for transfers between devices, local(): lax.psum_scatter(jnp.dot(grad_pre, w_up.T, preferred_element_type=jnp.flo...  41.1 us
    unnamed x1, blocking collectives  35.2 us
    reduce_scatter x1, waiting for transfers between devices, local(): lax.psum_scatter(jnp.dot(activation, w_down, preferred_element_type=jnp.f...  23.4 us
    all_gather x1, waiting for transfers between devices, local(): lax.all_gather(grad_mlp, 'mp', axis=0, tiled=True)  18 us
    all_gather x1, waiting for transfers between devices, local(): gathered = lax.all_gather(second_low, 'mp', axis=0, tiled=True)  16.4 us
    unnamed x127, local copies, waits for them, and re-layouts  11 us
  transfers between devices with their start and end apart: 9, of which 7 were waited for; matrix products, arithmetic and copies ran while one was open for 19% of the time, Pallas kernels for 0%

commit v1 on v0

v1 whole, which is shorter than its diff:
```python
import functools
import types

import jax
import jax.numpy as jnp
from jax import lax
from jax.experimental import pallas as pl
from jax.experimental.pallas import tpu as pltpu
from jax.sharding import PartitionSpec as P

HEADS = 12
EPSILON = 1e-06
LOW = jnp.bfloat16
F32 = jnp.float32
MESH = pl.DeviceIdType.MESH
VMEM_BYTES = 60 * 2**20
STAGES = 3


def mm(a, b, along_a=1, along_b=0):
    return lax.dot_general(a, b, (((along_a,), (along_b,)), ((), ())), preferred_element_type=F32)


def norm_rate(v):
    return lax.rsqrt(jnp.mean(v * v, axis=1, keepdims=True) + EPSILON)


def gelu_and_slope(v):
    c = 0.7978845608028654
    square = v * v
    t = jnp.tanh(v * (c + (c * 0.044715) * square))
    half = 0.5 + 0.5 * t
    slope = half + (0.5 * v) * (1.0 - t * t) * (c + (c * 3 * 0.044715) * square)
    return v * half, slope


def iota(shape, dim):
    return lax.broadcasted_iota(jnp.int32, shape, dim)


class Sizes:
    def __init__(self, rows, width, slots, hidden, batch):
        self.rows, self.width, self.slots, self.hidden, self.batch = rows, width, slots, hidden, batch
        self.block = width // batch
        self.folds = batch == 8 and self.block % 16 == 0
        self.part = width // STAGES


def scratch_of(s):
    n, d, f, c = s.slots, s.width, s.hidden, s.part
    tree = (2, 2, 2, s.block) if s.folds else (d,)
    found = dict(
        tok=pltpu.VMEM((s.rows, d), LOW),
        cot=pltpu.VMEM((s.rows, d), LOW),
        wqkv=pltpu.VMEM((d, 3 * d), LOW),
        wout=pltpu.VMEM((d, d), LOW),
        wup=pltpu.VMEM((2, d, f), LOW),
        wdn=pltpu.VMEM((2, f, d), LOW),
        pick=pltpu.VMEM((n, s.rows), LOW),
        picked=pltpu.VMEM((n, d), F32),
        cotr=pltpu.VMEM((n, d), LOW),
        first=pltpu.VMEM((n, d), LOW),
        qkv=pltpu.VMEM((n, 3 * d), LOW),
        bias=pltpu.VMEM((n, n), F32),
        probs=pltpu.VMEM((HEADS, n, n), LOW),
        mixed=pltpu.VMEM((n, d), LOW),
        attended=pltpu.VMEM((n, d), F32),
        resid=pltpu.VMEM((n, d), F32),
        sec=pltpu.VMEM((2, n, d), LOW),
        gm=pltpu.VMEM((2, n, d), LOW),
        act=pltpu.VMEM((2, 2 * n, f), LOW),
        gpre=pltpu.VMEM((2, 2 * n, f), LOW),
        gs_own=pltpu.VMEM((n, d), F32),
        mo_own=pltpu.VMEM((n, d), F32),
        gs_out=pltpu.VMEM((n, d), LOW),
        mo_out=pltpu.VMEM((n, d), LOW),
        gs_in=pltpu.VMEM((n, d), LOW),
        mo_in=pltpu.VMEM((n, d), LOW),
        gres=pltpu.VMEM((n, d), F32),
        gatt=pltpu.VMEM((n, d), LOW),
        gmix=pltpu.VMEM((n, d), LOW),
        dqkv=pltpu.VMEM((n, 3 * d), LOW),
        core_out=pltpu.VMEM((2, *tree, f), LOW),
        core_in=pltpu.VMEM((2, *tree, f), LOW),
        att=pltpu.VMEM((STAGES, 2, 2, *tree, c), LOW),
        att_core=pltpu.VMEM((STAGES, 2, *tree, c), LOW),
        att_x=pltpu.VMEM((STAGES, *tree, c), LOW),
        vec=pltpu.VMEM((6, 8, d), F32),
        vec_in=pltpu.VMEM((5, 8, d), F32),
        send_sem=pltpu.SemaphoreType.DMA((80,)),
        recv_sem=pltpu.SemaphoreType.DMA((80,)),
        local_sem=pltpu.SemaphoreType.DMA((8,)),
    )
    if s.folds:
        found |= dict(
            m0=pltpu.VMEM((2, 2, 2, s.block, f), LOW),
            m1=pltpu.VMEM((2, 2, s.block, f), LOW),
            m2=pltpu.VMEM((2, s.block, f), LOW),
            a0=pltpu.VMEM((STAGES, 2, 2, s.block, c), LOW),
            a1=pltpu.VMEM((STAGES, 2, s.block, c), LOW),
            a2=pltpu.VMEM((STAGES, s.block, c), LOW),
            ag=pltpu.VMEM((4, STAGES, s.block, c), LOW),
        )
    return found


def layer_kernel(s, names, *refs):
    ins, outs, scratch = refs[:12], refs[12:17], refs[17:]
    tokens, cotangent, key_mask, lengths, routed, w_router, gain_one, gain_two, w_qkv, w_out, w_up, w_down = ins
    upd_out, upd_tok, o_mlp, o_att, o_vec = outs
    v = types.SimpleNamespace(**dict(zip(names, scratch, strict=True)))
    n, d, f, c = s.slots, s.width, s.hidden, s.part
    half_rows = n // 2

    b, m = lax.axis_index("batch"), lax.axis_index("mp")
    lo, hi = m % 2, m // 2
    peer_lo, peer_hi, peer_far = (b, m + 1 - 2 * lo), (b, m + 2 - 4 * hi), (b, 3 - m)
    peers = [peer_lo, peer_hi, peer_far]
    if s.folds:
        y, zl, zh = b % 2, (b // 2) % 2, b // 4
        peer_y, peer_zl, peer_zh = (b + 1 - 2 * y, m), (b + 2 - 4 * zl, m), (b + 4 - 8 * zh, m)
        peers += [peer_y, peer_zl, peer_zh]

    barrier = pltpu.get_barrier_semaphore()
    for peer in peers:
        pl.semaphore_signal(barrier, inc=1, device_id=peer, device_id_type=MESH)

    sent = []

    def send(src, dst, peer):
        at = len(sent)
        copy = pltpu.make_async_remote_copy(
            src_ref=src,
            dst_ref=dst,
            send_sem=v.send_sem.at[at],
            recv_sem=v.recv_sem.at[at],
            device_id=peer,
            device_id_type=MESH,
        )
        copy.start()
        sent.append(copy)
        return copy

    fetches = []
    for src, dst in (
        (tokens.at[0], v.tok),
        (cotangent.at[0], v.cot),
        (w_qkv, v.wqkv),
        (w_out, v.wout),
        (w_up, v.wup.at[0]),
        (w_down, v.wdn.at[0]),
    ):
        fetches.append(pltpu.make_async_copy(src, dst, v.local_sem.at[len(fetches)]))
        fetches[-1].start()
    got_tok, got_cot, got_qkv, got_out, got_up, got_down = fetches

    live_count = lengths[0] // 8
    wanted = jnp.where(iota((1, n), 1) < live_count, routed[...], -1).astype(F32)
    on_diagonal = iota((n, n), 0) == iota((n, n), 1)
    wanted_column = jnp.sum(jnp.where(on_diagonal, wanted, 0.0), axis=1, keepdims=True).astype(jnp.int32)
    live = jnp.where(iota((n, 1), 0) < live_count, 1.0, 0.0)
    v.pick[...] = jnp.where(iota((n, s.rows), 1) == wanted_column, 1.0, 0.0).astype(LOW)

    got_tok.wait()
    picked = mm(v.pick[...], v.tok[...])
    v.picked[...] = picked
    router_row = w_router[...].astype(F32)
    one_row = gain_one[...].astype(F32)
    two_row = gain_two[...].astype(F32)
    gate_rate = 1.0 / (1.0 + jnp.exp(-jnp.sum(picked * router_row, axis=1, keepdims=True)))
    route_gain = live * gate_rate
    rate_one = norm_rate(picked)
    v.first[...] = (picked * rate_one * one_row).astype(LOW)

    got_cot.wait()
    cot_rows = mm(v.pick[...], v.cot[...])
    v.cotr[...] = cot_rows.astype(LOW)
    v.gm[0] = (route_gain * cot_rows).astype(LOW)

    pl.semaphore_wait(barrier, len(peers))
    sent_gm = send(v.gm.at[0], v.gm.at[1], peer_hi)
    sent_up = send(w_up, v.wup.at[1], peer_lo)
    sent_down = send(w_down, v.wdn.at[1], peer_lo)

    got_qkv.wait()
    for at in range(3 * STAGES):
        cols = slice(at * c, at * c + c)
        v.qkv[:, cols] = mm(v.first[...], v.wqkv[:, cols]).astype(LOW)

    mask_rows = jnp.broadcast_to(key_mask[...].astype(F32), (8, s.rows)).astype(LOW)
    key_open = mm(mask_rows, v.pick[...], 1, 1)[0:1] > 0.5
    earlier = iota((n, n), 1) < iota((n, n), 0)
    v.bias[...] = jnp.where((earlier & key_open) | on_diagonal, 0.0, -1e30)

    pair = 2 * (d // HEADS)
    lane = iota((n, pair), 1)
    side = [lane < pair // 2, lane >= pair // 2]

    def only(x, at):
        return jnp.where(side[at], x.astype(F32), 0.0).astype(LOW)

    def attend(p, _):
        at = pl.multiple_of(p * pair, pair)
        q, k, val = (v.qkv[:, pl.ds(pl.multiple_of(g * d + at, pair), pair)] for g in range(3))
        q = (q.astype(F32) * (d // HEADS) ** -0.5).astype(LOW)
        total = 0.0
        for h in range(2):
            scores = mm(only(q, h), k, 1, 1) + v.bias[...]
            powers = jnp.exp(scores - jnp.max(scores, axis=1, keepdims=True))
            probs = (powers * (1.0 / jnp.sum(powers, axis=1, keepdims=True))).astype(LOW)
            v.probs[2 * p + h] = probs
            total = total + mm(probs, only(val, h))
        v.mixed[:, pl.ds(at, pair)] = total.astype(LOW)
        return 0

    lax.fori_loop(0, HEADS // 2, attend, 0)

    got_out.wait()
    sent_sec = []
    for at in range(2):
        rows = slice(at * half_rows, (at + 1) * half_rows)
        attended = mm(v.mixed[rows], v.wout[...])
        v.attended[rows] = attended
        resid = v.picked[rows] + attended
        v.resid[rows] = resid
        v.sec[0, rows] = (resid * norm_rate(resid) * two_row).astype(LOW)
        sent_sec.append(send(v.sec.at[0, pl.ds(at * half_rows, half_rows)], v.sec.at[1, pl.ds(at * half_rows, half_rows)], peer_hi))

    got_up.wait()
    got_down.wait()

    def feed(j, start, count):
        x, g = v.sec[j, start : start + count], v.gm[j, start : start + count]
        gs, mo = 0.0, 0.0
        for w in range(2):
            rows = slice(j * n + start, j * n + start + count)
            act, slope = gelu_and_slope(mm(x, v.wup[w]))
            act = act.astype(LOW)
            v.act[w, rows] = act
            gpre = (mm(g, v.wdn[w], 1, 1) * slope).astype(LOW)
            v.gpre[w, rows] = gpre
            gs = gs + mm(gpre, v.wup[w], 1, 1)
            mo = mo + mm(act, v.wdn[w])
        return gs, mo

    sent_up.wait_recv()
    sent_down.wait_recv()
    for at in range(2):
        rows = slice(at * half_rows, (at + 1) * half_rows)
        v.gs_own[rows], v.mo_own[rows] = feed(0, at * half_rows, half_rows)

    sent_gm.wait_recv()
    sent_gs, sent_mo = [], []
    for at in range(2):
        rows = slice(at * half_rows, (at + 1) * half_rows)
        there = pl.ds(at * half_rows, half_rows)
        sent_sec[at].wait_recv()
        gs, mo = feed(1, at * half_rows, half_rows)
        v.gs_out[rows] = gs.astype(LOW)
        sent_gs.append(send(v.gs_out.at[there], v.gs_in.at[there], peer_hi))
        v.mo_out[rows] = mo.astype(LOW)
        sent_mo.append(send(v.mo_out.at[there], v.mo_in.at[there], peer_hi))

    def weight_grad(kind, w):
        left, right = (v.sec, v.gpre) if kind == 0 else (v.gm, v.act)
        return mm(left[...].reshape(2 * n, d), right[w], 0, 0)

    sent_core = []
    for kind in range(2):
        v.core_out[kind] = weight_grad(kind, 1).astype(LOW).reshape(v.core_out.shape[1:])
        sent_core.append(send(v.core_out.at[kind], v.core_in.at[kind], peer_lo))

    class Fold:
        def __init__(self, table, r0, r1, r2):
            self.table, self.r0, self.r1, self.r2 = table, r0, r1, r2

        def start_y(self):
            self.going = [send(self.table.at[at, :, 1 - y], self.r0.at[at], peer_y) for at in range(2)]

        def end_y(self):
            for copy in self.going:
                copy.wait_recv()
            for i in range(2):
                for j in range(2):
                    self.r0[i, j] = (self.r0[i, j].astype(F32) + self.table[i, j, y].astype(F32)).astype(LOW)
            self.going = [send(self.r0.at[:, 1 - zl], self.r1, peer_zl)]

        def end_zl(self):
            self.going[0].wait_recv()
            for i in range(2):
                self.r1[i] = (self.r1[i].astype(F32) + self.r0[i, zl].astype(F32)).astype(LOW)
            self.going = [send(self.r1.at[1 - zh], self.r2, peer_zh)]

        def end_zh(self):
            self.going[0].wait_recv()
            return self.r2[...].astype(F32) + self.r1[zh].astype(F32)

    mlp_folds = []
    for kind in range(2):
        own = weight_grad(kind, 0).reshape(v.core_in.shape[1:])
        sent_core[kind].wait_recv()
        v.core_in[kind] = (v.core_in[kind].astype(F32) + own).astype(LOW)
        if s.folds:
            fold = Fold(v.core_in.at[kind], v.m0.at[kind], v.m1.at[kind], v.m2.at[kind])
            fold.start_y()
            mlp_folds.append(fold)
        else:
            o_mlp[kind] = v.core_in[kind]

    gain_two_sum = 0.0
    for at in range(2):
        rows = slice(at * half_rows, (at + 1) * half_rows)
        sent_gs[at].wait_recv()
        gs = (v.gs_own[rows] + v.gs_in[rows].astype(F32)).astype(LOW).astype(F32)
        resid = v.resid[rows]
        rate = norm_rate(resid)
        gain_two_sum = gain_two_sum + jnp.sum(gs * (resid * rate), axis=0, keepdims=True)
        scaled = gs * two_row
        gres = rate * scaled - resid * (rate * rate * rate * jnp.mean(scaled * resid, axis=1, keepdims=True))
        v.gres[rows] = gres
        gatt = (route_gain[rows] * v.cotr[rows].astype(F32) + gres).astype(LOW)
        v.gatt[rows] = gatt
        v.gmix[rows] = mm(gatt, v.wout[...], 1, 1).astype(LOW)

    def attend_back(p, _):
        at = pl.multiple_of(p * pair, pair)
        where = [pl.ds(pl.multiple_of(g * d + at, pair), pair) for g in range(3)]
        q, k, val = (v.qkv[:, cols] for cols in where)
        gmix = v.gmix[:, pl.ds(at, pair)]
        gq, gk, gv = 0.0, 0.0, 0.0
        for h in range(2):
            probs = v.probs[2 * p + h]
            gmix_h = only(gmix, h)
            gprobs = mm(gmix_h, val, 1, 1)
            wide = probs.astype(F32)
            product = gprobs * wide
            gscores = product - wide * jnp.sum(product, axis=1, keepdims=True)
            gscores = (gscores * (d // HEADS) ** -0.5).astype(LOW)
            gq = gq + mm(gscores, only(k, h))
            gk = gk + mm(gscores, only(q, h), 0, 0)
            gv = gv + mm(probs, gmix_h, 0, 0)
        for cols, grad in zip(where, (gq, gk, gv), strict=True):
            v.dqkv[:, cols] = grad.astype(LOW)
        return 0

    att_core, att_x, att_folds = [], [], []

    def end_core(t):
        att_core[t].wait_recv()
        for i in range(2):
            v.att_core[t, i] = (v.att_core[t, i].astype(F32) + v.att[t, i, lo].astype(F32)).astype(LOW)
        att_x.append(send(v.att_core.at[t, 1 - hi], v.att_x.at[t], peer_hi))

    def end_x(t):
        att_x[t].wait_recv()
        v.att_x[t] = (v.att_x[t].astype(F32) + v.att_core[t, hi].astype(F32)).astype(LOW)
        if s.folds:
            fold = Fold(v.att_x.at[t], v.a0.at[t], v.a1.at[t], v.a2.at[t])
            fold.start_y()
            att_folds.append(fold)
        else:
            o_att[t] = v.att_x[t]

    for t in range(STAGES):
        lax.fori_loop(t * HEADS // 2 // STAGES, (t + 1) * HEADS // 2 // STAGES, attend_back, 0)
        for g in range(4):
            if g < 3:
                left, right = v.first[...], v.dqkv[:, g * d + t * c : g * d + t * c + c]
            else:
                left, right = v.mixed[...], v.gatt[:, t * c : t * c + c]
            v.att[t, g // 2, g % 2] = mm(left, right, 0, 0).astype(LOW).reshape(v.att.shape[3:])
        att_core.append(send(v.att.at[t, :, 1 - lo], v.att_core.at[t], peer_lo))
        if t > 0:
            end_core(t - 1)
        if s.folds and t > 0:
            mlp_folds[t - 1].end_y()
    end_core(STAGES - 1)

    gfirst = mm(v.dqkv[...], v.wqkv[...], 1, 1)
    picked = v.picked[...]
    gain_one_sum = jnp.sum(gfirst * (picked * rate_one), axis=0, keepdims=True)
    scaled = gfirst * one_row
    gnorm = rate_one * scaled - picked * (rate_one * rate_one * rate_one * jnp.mean(scaled * picked, axis=1, keepdims=True))
    for copy in sent_mo:
        copy.wait_recv()
    branch = v.attended[...] + (v.mo_own[...] + v.mo_in[...].astype(F32)).astype(LOW).astype(F32)
    grate = live * jnp.sum(v.cotr[...].astype(F32) * branch, axis=1, keepdims=True)
    glogit = grate * gate_rate * (1.0 - gate_rate)
    router_sum = jnp.sum(glogit * picked, axis=0, keepdims=True)
    upd_out[...] = (route_gain * branch).astype(LOW)
    upd_tok[...] = (live * (gnorm + v.gres[...] + glogit * router_row)).astype(LOW)

    row = iota((8, d), 0)
    v.vec[0] = jnp.where(row == 0, router_sum, jnp.where(row == 1, gain_one_sum, jnp.where(row == 2, gain_two_sum, 0.0)))
    vec_peers = [peer_lo, peer_hi] + ([peer_y, peer_zl, peer_zh] if s.folds else [])
    vec_going = []

    def vec_step():
        at = len(vec_going)
        if at:
            vec_going[-1].wait_recv()
            v.vec[at] = v.vec[at - 1] + v.vec_in[at - 1]
        if at < len(vec_peers):
            vec_going.append(send(v.vec.at[at], v.vec_in.at[at], vec_peers[at]))

    vec_step()
    if s.folds:
        mlp_folds[0].end_zl()
        mlp_folds[1].end_zl()
    end_x(0)
    vec_step()
    if s.folds:
        o_mlp[0] = mlp_folds[0].end_zh()
        o_mlp[1] = mlp_folds[1].end_zh()
    end_x(1)
    if s.folds:
        att_folds[0].end_y()
        vec_step()
    end_x(2)
    if s.folds:
        gathers = []

        def end_zh(t):
            v.ag[m, t] = att_folds[t].end_zh().astype(LOW)
            for peer in (peer_lo, peer_hi, peer_far):
                gathers.append(send(v.ag.at[m, t], v.ag.at[m, t], peer))

        att_folds[0].end_zl()
        att_folds[1].end_y()
        vec_step()
        att_folds[1].end_zl()
        end_zh(0)
        att_folds[2].end_y()
        vec_step()
        end_zh(1)
        att_folds[2].end_zl()
        end_zh(2)
        for copy in gathers:
            copy.wait_recv()
        o_att[...] = v.ag[...]
    vec_step()
    o_vec[...] = v.vec[len(vec_peers)]
    for copy in sent:
        copy.wait_send()


def spread_kernel(lengths, routed, tokens, cotangent, upd_out, upd_tok, mlp, att, vec, block_out, grad_tokens, g_up, g_down, g_qkv, g_out, g_vec):
    step = pl.program_id(0)
    rows, n = tokens.shape[1], routed.shape[1]
    block, d = g_out.shape
    wanted = jnp.where(iota((1, n), 1) < lengths[0] // 8, routed[...], -1)
    place = jnp.where(iota((rows, n), 0) + step * rows == wanted, 1.0, 0.0).astype(LOW)
    block_out[0] = (tokens[0].astype(F32) + mm(place, upd_out[...])).astype(LOW)
    grad_tokens[0] = (cotangent[0].astype(F32) + mm(place, upd_tok[...])).astype(LOW)

    @pl.when(step == 0)
    def _():
        g_up[...] = mlp[0]
        g_down[...] = mlp[1].T
        part = att.shape[3]
        for g in range(4):
            for t in range(att.shape[1]):
                piece = att[g, t].astype(F32)
                if g < 3:
                    g_qkv[:, g * d + t * part : g * d + (t + 1) * part] = piece
                else:
                    g_out[:, t * part : (t + 1) * part] = piece
        mine = iota((d, g_vec.shape[1]), 0) == iota((d, g_vec.shape[1]), 1) + lax.axis_index("batch") * block
        g_vec[...] = lax.dot_general(
            vec[...], jnp.where(mine, 1.0, 0.0), (((1,), (0,)), ((), ())),
            preferred_element_type=F32, precision=lax.Precision.HIGHEST,
        )


def local(tokens, key_mask, lengths, routed, w_router, gain_one, gain_two, w_qkv, w_out, w_up, w_down, cotangent):
    _, rows, d = tokens.shape
    n, f = routed.shape[1], w_up.shape[1]
    batch, mp = lax.axis_size("batch"), lax.axis_size("mp")
    s = Sizes(rows, d, n, f, batch)
    found = scratch_of(s)
    vmem, smem, anywhere = (pl.BlockSpec(memory_space=space) for space in (pltpu.VMEM, pltpu.SMEM, pl.ANY))
    if s.folds:
        mlp_shape, att_shape = jax.ShapeDtypeStruct((2, s.block, f), F32), jax.ShapeDtypeStruct((4, STAGES, s.block, s.part), LOW)
    else:
        mlp_shape, att_shape = jax.ShapeDtypeStruct((2, d, f), LOW), jax.ShapeDtypeStruct((STAGES, d, s.part), LOW)
    upd_out, upd_tok, mlp, att, vec = pl.pallas_call(
        functools.partial(layer_kernel, s, tuple(found)),
        out_shape=(
            jax.ShapeDtypeStruct((n, d), LOW),
            jax.ShapeDtypeStruct((n, d), LOW),
            mlp_shape,
            att_shape,
            jax.ShapeDtypeStruct((8, d), F32),
        ),
        in_specs=[anywhere, anywhere, vmem, smem, vmem, vmem, vmem, vmem, anywhere, anywhere, anywhere, anywhere],
        out_specs=[vmem] * 5,
        scratch_shapes=list(found.values()),
        compiler_params=pltpu.CompilerParams(collective_id=0, has_side_effects=True, vmem_limit_bytes=VMEM_BYTES),
        name="layer",
    )(
        tokens, cotangent, key_mask, lengths, routed,
        w_router.reshape(1, d), gain_one.reshape(1, d), gain_two.reshape(1, d),
        w_qkv, w_out, w_up, w_down,
    )
    if not s.folds:
        mlp = lax.psum_scatter(mlp.astype(F32), "batch", scatter_dimension=1, tiled=True)
        att = lax.psum_scatter(att.astype(F32), "batch", scatter_dimension=1, tiled=True).astype(LOW)
        att = lax.all_gather(att, "mp", axis=0)
        vec = lax.psum(vec, "batch")
    tile = rows // 4
    tiles = pl.BlockSpec((1, tile, d), lambda i: (0, i, 0))
    block_out, grad_tokens, g_up, g_down, g_qkv, g_out, g_vec = pl.pallas_call(
        spread_kernel,
        grid=(rows // tile,),
        out_shape=(
            jax.ShapeDtypeStruct(tokens.shape, LOW),
            jax.ShapeDtypeStruct(tokens.shape, LOW),
            jax.ShapeDtypeStruct((s.block, f), F32),
            jax.ShapeDtypeStruct((f, s.block), F32),
            jax.ShapeDtypeStruct((s.block, 3 * d), F32),
            jax.ShapeDtypeStruct((s.block, d), F32),
            jax.ShapeDtypeStruct((8, s.block), F32),
        ),
        in_specs=[smem, vmem, tiles, tiles, vmem, vmem, vmem, vmem, vmem],
        out_specs=[tiles, tiles, vmem, vmem, vmem, vmem, vmem],
        compiler_params=pltpu.CompilerParams(vmem_limit_bytes=VMEM_BYTES),
        name="spread",
    )(lengths, routed, tokens, cotangent, upd_out, upd_tok, mlp, att, vec)
    return block_out, grad_tokens, g_vec[0], g_vec[1], g_vec[2], g_qkv, g_out, g_up, g_down


def solution(mesh):
    rows_spec = P(("batch", "mp"), None, None)
    in_specs = (
        rows_spec,
        P(("batch", "mp"), None),
        P(("batch", "mp")),
        P(("batch", "mp"), None),
        P(),
        P(),
        P(),
        P(),
        P(),
        P(None, "mp"),
        P("mp", None),
        rows_spec,
    )
    out_specs = (
        rows_spec,
        rows_spec,
        P("batch"),
        P("batch"),
        P("batch"),
        P("batch", None),
        P("batch", None),
        P("batch", "mp"),
        P("mp", "batch"),
    )
    return jax.shard_map(local, mesh=mesh, in_specs=in_specs, out_specs=out_specs, check_vma=False)
```

time: 476 us -> 123 us (0.26)
  waiting for transfers between devices: 244 us -> 0 us
  Pallas kernels: 0 us -> 115 us
  other arithmetic: 72.9 us -> 0 us
  matrix products: 57.8 us -> 0 us
  blocking collectives: 41.5 us -> 0 us
  local copies, waits for them, and re-layouts: 31.2 us -> 6.97 us
  between operations: 16.1 us -> 1.3 us
  starting transfers between devices: 10.9 us -> 0 us
    reduce_scatter x4 -> x0, waiting for transfers between devices: 160 us -> none  [the longest x1 95.6 us: local(): lax.psum_scatter(grad_qkv_local, 'batch', scatter_dimension=0, tiled=True)]
    pallas_call x0 -> x2, Pallas kernels: none -> 115 us  [the longest x1 106 us: local(): pl.pallas_call(functools.partial(layer_kernel, s, tuple(found)), out_shap...]
    dot_general x19 -> x0, matrix products: 57.8 us -> none  [the longest x1 6.88 us: local(): pre_act = jnp.dot(gathered, w_up, preferred_element_type=jnp.float32)]
    all_to_all x2 -> x0, waiting for transfers between devices: 49.2 us -> none  [sum_at_owner(): lax.all_to_all(blocks, axis, split_axis=0, concat_axis=0, tiled=True)]
    unnamed x1 -> x0, blocking collectives: 35.2 us -> none
    all_gather x2 -> x0, waiting for transfers between devices: 34.4 us -> none  [the longest x1 18 us: local(): lax.all_gather(grad_mlp, 'mp', axis=0, tiled=True)]
    convert_element_type x15 -> x0, other arithmetic: 23.1 us -> none  [the longest x1 5.27 us: local(): seq_tokens.astype(jnp.float32).at[select_ids]]
    scatter-add x2 -> x0, other arithmetic: 18.3 us -> none  [the longest x1 9.4 us: local(): cotangent[0].astype(jnp.float32).at[select_ids]]
  transfers between devices with their start and end apart: 9 -> 0, of which waited for: 7 -> 0; matrix products, arithmetic and copies ran while one was open for 19% -> 0% of each run, Pallas kernels for 0% -> 0%
where the time goes in v1:
time: 123 us
  Pallas kernels  115 us (93%)
  local copies, waits for them, and re-layouts  6.97 us (6%)
  between operations  1.3 us (1%)
    pallas_call x1, Pallas kernels, local(): pl.pallas_call(functools.partial(layer_kernel, s, tuple(found)), out_shap...  106 us
    pallas_call x1, Pallas kernels, local(): pl.pallas_call(spread_kernel, grid=(rows // tile,), out_shape=(jax.ShapeD...  8.48 us

profile of v1, /device:TPU:0, one launch (start us, length us, event | category | flops | bytes accessed | tf_op | source)
XLA Modules:
  0.0 122.8 jit_solution(5787059247142220203)
XLA Ops:
  1.3 1.3 %reshape.27.refs_5_ = bf16[1,768]{1,0:T(2,128)(2,1)} reshape(bf16[768]{0:T(1024)(128)(2,1)} %param.16) | data formatting | bytes 3072 | tf_op jit(solution)/shard_map/reshape | solution.py:502
  2.6 1.3 %reshape.28.refs_6_ = bf16[1,768]{1,0:T(2,128)(2,1)} reshape(bf16[768]{0:T(1024)(128)(2,1)} %param.17) | data formatting | bytes 3072 | tf_op jit(solution)/shard_map/reshape | solution.py:502
  3.8 1.3 %reshape.29.refs_7_ = bf16[1,768]{1,0:T(2,128)(2,1)} reshape(bf16[768]{0:T(1024)(128)(2,1)} %param.18) | data formatting | bytes 3072 | tf_op jit(solution)/shard_map/reshape | solution.py:502
  5.1 106.1 %layer.1 = (bf16[256,768]{1,0:T(8,128)(2,1)}, bf16[256,768]{1,0:T(8,128)(2,1)}, f32[2,96,768]{2,1,0:T(8,128)}, bf16[4,3,96,256]{3,2,1,0:T(8,128)(2,1)}, f32[8,768]{1,0:T(8,128)}) custom-call(bf16[1,2048,768]{2,1,0:T(8,128)(2,1)} %tokens.1, bf16[1,2048,768]{2,1,0:T(8,128)(2,1)} %cotangent.1, s32[1,2048]{1,0:T(1,128)} %refs_2_.1, s32[1]{0:T(128)S(6)} %copy.22.refs_3_.lengths, ...), custom_call_target="tpu_custom_call" | custom-call | tf_op jit(solution)/shard_map/layer/pallas_call | solution.py:486
  111.2 8.5 %spread.1 = (bf16[1,2048,768]{2,1,0:T(8,128)(2,1)}, bf16[1,2048,768]{2,1,0:T(8,128)(2,1)}, f32[96,768]{1,0:T(8,128)}, f32[768,96]{1,0:T(8,128)}, f32[96,2304]{1,...) custom-call(s32[1]{0:T(128)S(6)} %copy.22.refs_3_.lengths, s32[1,256]{1,0:T(1,128)} %routed.1, ...), custom_call_target="tpu_custom_call" | custom-call | tf_op jit(solution)/shard_map/spread/pallas_call | solution.py:512
  119.7 1.3 %slice_bitcast_fusion = (f32[96]{0:T(128)}, f32[96]{0:T(128)}, f32[96]{0:T(128)}) fusion(f32[8,96]{1,0:T(8,128)} %get-tuple-element.28), kind=kLoop, calls=%fused_computation | loop fusion | bytes 2304 | tf_op jit(solution)/shard_map/squeeze | solution.py:529
  121.0 1.9 %copy.21 = f32[768,96]{0,1:T(8,128)} copy(f32[768,96]{1,0:T(8,128)} %get-tuple-element.41) | data formatting | bytes 589824

commit v2 on v1

v2 whole, which is shorter than its diff:
```python
import functools
import itertools
import types

import jax
import jax.numpy as jnp
from jax import lax
from jax.experimental import pallas as pl
from jax.experimental.pallas import tpu as pltpu
from jax.sharding import PartitionSpec as P

HEADS = 12
EPSILON = 1e-06
LOW = jnp.bfloat16
F32 = jnp.float32
MESH = pl.DeviceIdType.MESH
VMEM_BYTES = 54 * 2**20
AXES = "dxbay"
MLP_ORDERS = ("ayb", "yab", "yab", "yab", "yab", "aby")
ATT_ORDERS = ("dxyab", "dxyab", "dxyab", "daxyb", "dyxab", "dxyab")
SEQUENCE = (
    ("f0", "f1", "u0", "u1", "u2", "u3", "u4", "u5", "w0", "w1", "w2", "w3", "w4", "w5", "r0", "r1", "b0", "m0", "m1"),
    ("b1", "a0", "b2", "a1", "m5", "m2", "b3", "a2", "m1", "b4", "a3", "m3", "b5", "a4", "a0", "m2", "m5", "e0", "a5"),
    ("m4", "m1", "e1", "a1", "m0", "a3", "v", "s0", "m3", "a4", "s1", "a2", "m2", "s2", "s3", "a0", "m4", "m5", "a5", "m0", "a1", "a0", "a3"),
    ("m3", "v", "a2", "a1", "m4", "a4", "a5", "a0", "a3", "a2", "v", "a1", "a4", "a0", "a5", "a0", "a1", "a3", "v"),
    ("a1", "a2", "a4", "a3", "a5", "a2", "a3", "v", "a4", "a2", "a5", "a4", "a5"),
)


def mm(a, b, along_a=1, along_b=0):
    return lax.dot_general(a, b, (((along_a,), (along_b,)), ((), ())), preferred_element_type=F32)


def norm_rate(v):
    return lax.rsqrt(jnp.mean(v * v, axis=1, keepdims=True) + EPSILON)


def gelu_and_slope(v):
    c = 0.7978845608028654
    square = v * v
    t = jnp.tanh(v * (c + (c * 0.044715) * square))
    half = 0.5 + 0.5 * t
    slope = half + (0.5 * v) * (1.0 - t * t) * (c + (c * 3 * 0.044715) * square)
    return v * half, slope


def iota(shape, dim):
    return lax.broadcasted_iota(jnp.int32, shape, dim)


class Sizes:
    def __init__(self, rows, width, slots, hidden, batch):
        self.rows, self.width, self.slots, self.hidden, self.batch = rows, width, slots, hidden, batch
        self.block = width // batch
        self.folds = batch == 8 and self.block % 16 == 0
        self.pair = 2 * (width // HEADS)
        self.pairs = HEADS // 2
        self.part = hidden // 3
        self.mlp_orders = MLP_ORDERS if self.folds else ("",) * len(MLP_ORDERS)
        self.att_orders = ATT_ORDERS if self.folds else ("dx",) * len(ATT_ORDERS)
        self.tail = (self.block,) if self.folds else (width,)

    def table(self, axes, columns):
        return (*(2 for axis in AXES if axis in axes), *self.tail, columns)


def scratch_of(s):
    n, d, f = s.slots, s.width, s.hidden
    found = dict(
        cot=pltpu.VMEM((s.rows, d), LOW),
        wqkv=pltpu.VMEM((d, 3 * d), LOW),
        wout=pltpu.VMEM((d, d), LOW),
        wup=pltpu.VMEM((2, d, f), LOW),
        wdn=pltpu.VMEM((2, f, d), LOW),
        pick=pltpu.VMEM((n, s.rows), LOW),
        picked=pltpu.VMEM((n, d), F32),
        cotr=pltpu.VMEM((n, d), LOW),
        first=pltpu.VMEM((n, d), LOW),
        qkv=pltpu.VMEM((n, 3 * d), LOW),
        bias=pltpu.VMEM((n, n), F32),
        probs=pltpu.VMEM((HEADS, n, n), LOW),
        mixed=pltpu.VMEM((n, d), LOW),
        first_t=pltpu.VMEM((d, n), LOW),
        mixed_t=pltpu.VMEM((d, n), LOW),
        sec_t=pltpu.VMEM((d, 2 * n), LOW),
        upd_out=pltpu.VMEM((n, d), LOW),
        upd_tok=pltpu.VMEM((n, d), LOW),
        gm_t=pltpu.VMEM((d, 2 * n), LOW),
        attended=pltpu.VMEM((n, d), F32),
        resid=pltpu.VMEM((n, d), F32),
        sec=pltpu.VMEM((2, n, d), LOW),
        gm=pltpu.VMEM((2, n, d), LOW),
        act=pltpu.VMEM((2, 2 * n, f), LOW),
        gpre=pltpu.VMEM((2, 2 * n, f), LOW),
        gs_own=pltpu.VMEM((n, d), F32),
        mo_own=pltpu.VMEM((n, d), F32),
        gs_out=pltpu.VMEM((n, d), LOW),
        mo_out=pltpu.VMEM((n, d), LOW),
        gs_in=pltpu.VMEM((n, d), LOW),
        mo_in=pltpu.VMEM((n, d), LOW),
        gres=pltpu.VMEM((n, d), F32),
        gatt=pltpu.VMEM((n, d), LOW),
        gmix=pltpu.VMEM((n, d), LOW),
        dqkv=pltpu.VMEM((n, 3 * d), LOW),
        vec=pltpu.VMEM((6, 8, d), F32),
        vec_in=pltpu.VMEM((5, 8, d), F32),
        send_sem=pltpu.SemaphoreType.DMA((112,)),
        recv_sem=pltpu.SemaphoreType.DMA((112,)),
        local_sem=pltpu.SemaphoreType.DMA((16,)),
    )
    batch_axes = "bay" if s.folds else ""
    for name, orders, axes, columns in (("m", s.mlp_orders, batch_axes, s.part), ("a", s.att_orders, "dx" + batch_axes, s.pair)):
        for at, order in enumerate(orders):
            left = axes
            found[f"{name}{at}_0"] = pltpu.VMEM(s.table(left, columns), LOW)
            for step, axis in enumerate(order):
                left = left.replace(axis, "")
                found[f"{name}{at}_{step + 1}"] = pltpu.VMEM(s.table(left, columns), LOW)
            if name == "m":
                found[f"u{at}"] = pltpu.VMEM(s.table(axes, columns), LOW)
    if s.folds:
        found["gathered"] = pltpu.VMEM((4, s.pairs, s.block, s.pair), LOW)
    return found


def layer_kernel(s, names, *refs):
    ins, outs, scratch = refs[:12], refs[12:21], refs[21:]
    tokens, cotangent, key_mask, lengths, routed, w_router, gain_one, gain_two, w_qkv, w_out, w_up, w_down = ins
    block_out, grad_tokens, o_up, o_down, o_qkv, o_out, *o_vecs = outs
    v = types.SimpleNamespace(**dict(zip(names, scratch, strict=True)), tok=block_out.at[0])
    n, d, f, pair = s.slots, s.width, s.hidden, s.pair
    half_rows = n // 2

    b, m = lax.axis_index("batch"), lax.axis_index("mp")
    lo, hi = m % 2, m // 2
    here = {"d": lo, "x": hi}
    peer = {"d": (b, m + 1 - 2 * lo), "x": (b, m + 2 - 4 * hi)}
    if s.folds:
        y, zl, zh = b % 2, (b // 2) % 2, b // 4
        here |= {"y": y, "a": zl, "b": zh}
        peer |= {"y": (b + 1 - 2 * y, m), "a": (b + 2 - 4 * zl, m), "b": (b + 4 - 8 * zh, m)}

    barrier = pltpu.get_barrier_semaphore()
    for other in peer.values():
        pl.semaphore_signal(barrier, inc=1, device_id=other, device_id_type=MESH)

    sent = []

    def send(src, dst, axis):
        at = len(sent)
        copy = pltpu.make_async_remote_copy(
            src_ref=src,
            dst_ref=dst,
            send_sem=v.send_sem.at[at],
            recv_sem=v.recv_sem.at[at],
            device_id=peer[axis],
            device_id_type=MESH,
        )
        copy.start()
        sent.append(copy)
        return copy

    fetches = []
    for src, dst in (
        (tokens.at[0], v.tok),
        (cotangent.at[0], v.cot),
        (w_qkv, v.wqkv),
        (w_out, v.wout),
        (w_up, v.wup.at[0]),
        (w_down, v.wdn.at[0]),
    ):
        fetches.append(pltpu.make_async_copy(src, dst, v.local_sem.at[len(fetches)]))
        fetches[-1].start()
    got_tok, got_cot, got_qkv, got_out, got_up, got_down = fetches

    live_count = lengths[0] // 8
    wanted = jnp.where(iota((1, n), 1) < live_count, routed[...], -1).astype(F32)
    on_diagonal = iota((n, n), 0) == iota((n, n), 1)
    wanted_column = jnp.sum(jnp.where(on_diagonal, wanted, 0.0), axis=1, keepdims=True).astype(jnp.int32)
    live = jnp.where(iota((n, 1), 0) < live_count, 1.0, 0.0)
    v.pick[...] = jnp.where(iota((n, s.rows), 1) == wanted_column, 1.0, 0.0).astype(LOW)

    got_tok.wait()
    picked = mm(v.pick[...], v.tok[...])
    v.picked[...] = picked
    router_row, one_row, two_row = (row[...].astype(F32).reshape(1, d) for row in (w_router, gain_one, gain_two))
    gate_rate = 1.0 / (1.0 + jnp.exp(-jnp.sum(picked * router_row, axis=1, keepdims=True)))
    route_gain = live * gate_rate

    got_cot.wait()
    cot_rows = mm(v.pick[...], v.cot[...])
    v.gm[0] = (route_gain * cot_rows).astype(LOW)

    pl.semaphore_wait(barrier, len(peer))
    sent_gm = send(v.gm.at[0], v.gm.at[1], "x")
    sent_up = send(w_up, v.wup.at[1], "d")
    sent_down = send(w_down, v.wdn.at[1], "d")

    v.cotr[...] = cot_rows.astype(LOW)
    rate_one = norm_rate(picked)
    v.first[...] = (picked * rate_one * one_row).astype(LOW)
    got_qkv.wait()
    for at in range(0, 3 * d, 256):
        v.qkv[:, at : at + 256] = mm(v.first[...], v.wqkv[:, at : at + 256]).astype(LOW)

    mask_rows = jnp.broadcast_to(key_mask[...].astype(F32), (8, s.rows)).astype(LOW)
    key_open = mm(mask_rows, v.pick[...], 1, 1)[0:1] > 0.5
    earlier = iota((n, n), 1) < iota((n, n), 0)
    v.bias[...] = jnp.where((earlier & key_open) | on_diagonal, 0.0, -1e30)

    lane = iota((n, pair), 1)
    side = [lane < pair // 2, lane >= pair // 2]

    def only(x, at):
        return jnp.where(side[at], x.astype(F32), 0.0).astype(LOW)

    for p in range(s.pairs):
        q, k, val = (v.qkv[:, g * d + p * pair : g * d + (p + 1) * pair] for g in range(3))
        q = (q.astype(F32) * (d // HEADS) ** -0.5).astype(LOW)
        total = 0.0
        for h in range(2):
            scores = mm(only(q, h), k, 1, 1) + v.bias[...]
            powers = jnp.exp(scores - jnp.max(scores, axis=1, keepdims=True))
            probs = (powers * (1.0 / jnp.sum(powers, axis=1, keepdims=True))).astype(LOW)
            v.probs[2 * p + h] = probs
            total = total + mm(probs, only(val, h))
        v.mixed[:, p * pair : (p + 1) * pair] = total.astype(LOW)

    got_out.wait()
    sent_sec = []
    for at in range(2):
        rows = slice(at * half_rows, (at + 1) * half_rows)
        there = pl.ds(at * half_rows, half_rows)
        attended = mm(v.mixed[rows], v.wout[...])
        v.attended[rows] = attended
        resid = v.picked[rows] + attended
        v.resid[rows] = resid
        v.sec[0, rows] = (resid * norm_rate(resid) * two_row).astype(LOW)
        sent_sec.append(send(v.sec.at[0, there], v.sec.at[1, there], "x"))

    got_up.wait()
    got_down.wait()

    def feed(j, start, count):
        x, g = v.sec[j, start : start + count], v.gm[j, start : start + count]
        gs, mo = 0.0, 0.0
        for w in range(2):
            rows = slice(j * n + start, j * n + start + count)
            act, slope = gelu_and_slope(mm(x, v.wup[w]))
            act = act.astype(LOW)
            v.act[w, rows] = act
            gpre = (mm(g, v.wdn[w], 1, 1) * slope).astype(LOW)
            v.gpre[w, rows] = gpre
            gs = gs + mm(gpre, v.wup[w], 1, 1)
            mo = mo + mm(act, v.wdn[w])
        return gs, mo

    sent_up.wait_recv()
    sent_down.wait_recv()
    v.gs_own[...], v.mo_own[...] = feed(0, 0, n)
    v.first_t[...] = v.first[...].T
    v.mixed_t[...] = v.mixed[...].T
    v.sec_t[:, :n] = v.sec[0].T
    v.gm_t[:, :n] = v.gm[0].T

    sent_gm.wait_recv()
    v.gm_t[:, n:] = v.gm[1].T
    sent_gs, sent_mo = [], []

    def feed_other(at):
        rows = slice(at * half_rows, (at + 1) * half_rows)
        there = pl.ds(at * half_rows, half_rows)
        sent_sec[at].wait_recv()
        gs, mo = feed(1, at * half_rows, half_rows)
        v.gs_out[rows] = gs.astype(LOW)
        sent_gs.append(send(v.gs_out.at[there], v.gs_in.at[there], "x"))
        v.mo_out[rows] = mo.astype(LOW)
        if at == 1:
            v.sec_t[:, n:] = v.sec[1].T
            for late in range(2):
                there = pl.ds(late * half_rows, half_rows)
                sent_mo.append(send(v.mo_out.at[there], v.mo_in.at[there], "x"))

    def weight_grad(at, w):
        left, right = (v.sec_t, v.gpre) if at < 3 else (v.gm_t, v.act)
        cols = slice(at % 3 * s.part, (at % 3 + 1) * s.part)
        return mm(left[...], right[w, :, cols])

    sent_core = []

    def other_core(at):
        table = getattr(v, f"u{at}")
        table[...] = weight_grad(at, 1).astype(LOW).reshape(table.shape)
        sent_core.append(send(table, getattr(v, f"m{at}_0"), "d"))

    class Sum:
        def __init__(self, name, axes, order, finish):
            self.name, self.axes, self.order, self.finish, self.at = name, axes, order, finish, 0
            if order:
                self.start()

        def table(self, at):
            return getattr(v, f"{self.name}_{at}")

        def start(self):
            axis = self.order[self.at]
            src = self.table(self.at).at[tuple(1 - here[k] if k == axis else slice(None) for k in self.axes)]
            self.going = send(src, self.table(self.at + 1), axis)

        def advance(self):
            if self.at == len(self.order):
                self.finish.advance()
                return
            axis = self.order[self.at]
            self.going.wait_recv()
            kept, arrived = self.table(self.at), self.table(self.at + 1)
            last = self.at + 1 == len(self.order)
            rest = self.axes.replace(axis, "")
            for index in itertools.product(*[range(2)] * len(rest)):
                full = dict(zip(rest, index, strict=True)) | {axis: here[axis]}
                total = arrived[index].astype(F32) + kept[tuple(full[k] for k in self.axes)].astype(F32)
                if last:
                    self.finish.begin(total)
                else:
                    arrived[index] = total.astype(LOW)
            self.axes, self.at = rest, self.at + 1
            if not last:
                self.start()

    class Store:
        def __init__(self, at):
            self.at = at

        def begin(self, total):
            out = o_up if self.at < 3 else o_down
            out[:, self.at % 3 * s.part : (self.at % 3 + 1) * s.part] = total

    class Gather:
        def __init__(self, p):
            self.p = p

        def begin(self, total):
            if not s.folds:
                o_qkv[self.p] = total
                return
            piece = v.gathered.at[m, self.p]
            piece[...] = total.astype(LOW)
            self.over_x = send(piece, piece, "x")
            self.over_d = send(piece, piece, "d")
            self.handed_on = None

        def advance(self):
            if self.handed_on is None:
                self.over_x.wait_recv()
                piece = v.gathered.at[m + 2 - 4 * hi, self.p]
                self.handed_on = send(piece, piece, "d")
            else:
                self.over_d.wait_recv()
                self.handed_on.wait_recv()
                for g in range(3):
                    o_qkv[:, g * d + self.p * pair : g * d + (self.p + 1) * pair] = v.gathered[g, self.p].astype(F32)
                o_out[:, self.p * pair : (self.p + 1) * pair] = v.gathered[3, self.p].astype(F32)

    sums = {}

    def own_core(at):
        own = weight_grad(at, 0)
        sent_core[at].wait_recv()
        table = getattr(v, f"m{at}_0")
        table[...] = (table[...].astype(F32) + own.reshape(table.shape)).astype(LOW)
        if s.folds:
            sums[f"m{at}"] = Sum(f"m{at}", "bay", s.mlp_orders[at], Store(at))
        else:
            out = o_up if at < 3 else o_down
            out[:, at % 3 * s.part : (at % 3 + 1) * s.part] = table[...].astype(F32)

    gain_two_sums = []

    def second_back(at):
        rows = slice(at * half_rows, (at + 1) * half_rows)
        sent_gs[at].wait_recv()
        gs = (v.gs_own[rows] + v.gs_in[rows].astype(F32)).astype(LOW).astype(F32)
        resid = v.resid[rows]
        rate = norm_rate(resid)
        gain_two_sums.append(jnp.sum(gs * (resid * rate), axis=0, keepdims=True))
        scaled = gs * two_row
        gres = rate * scaled - resid * (rate * rate * rate * jnp.mean(scaled * resid, axis=1, keepdims=True))
        v.gres[rows] = gres
        gatt = (route_gain[rows] * v.cotr[rows].astype(F32) + gres).astype(LOW)
        v.gatt[rows] = gatt
        v.gmix[rows] = mm(gatt, v.wout[...], 1, 1).astype(LOW)

    def attend_back(p):
        where = [slice(g * d + p * pair, g * d + (p + 1) * pair) for g in range(3)]
        q, k, val = (v.qkv[:, cols] for cols in where)
        gmix = v.gmix[:, p * pair : (p + 1) * pair]
        gq, gk, gv = 0.0, 0.0, 0.0
        for h in range(2):
            probs = v.probs[2 * p + h]
            gmix_h = only(gmix, h)
            gprobs = mm(gmix_h, val, 1, 1)
            wide = probs.astype(F32)
            product = gprobs * wide
            gscores = product - wide * jnp.sum(product, axis=1, keepdims=True)
            gscores = (gscores * (d // HEADS) ** -0.5).astype(LOW)
            gq = gq + mm(gscores, only(k, h))
            gk = gk + mm(gscores, only(q, h), 0, 0)
            gv = gv + mm(probs, gmix_h, 0, 0)
        table = getattr(v, f"a{p}_0")
        lower = []
        for cols, grad in zip(where, (gq, gk, gv), strict=True):
            lower.append(grad.astype(LOW))
            v.dqkv[:, cols] = lower[-1]
        both = mm(v.first_t[...], jnp.concatenate(lower[:2], axis=1)).astype(LOW)
        shape = table.shape[2:]
        table[0, 0] = both[:, :pair].reshape(shape)
        table[1, 0] = both[:, pair:].reshape(shape)
        table[0, 1] = mm(v.first_t[...], lower[2]).astype(LOW).reshape(shape)
        table[1, 1] = mm(v.mixed_t[...], v.gatt[:, p * pair : (p + 1) * pair]).astype(LOW).reshape(shape)
        sums[f"a{p}"] = Sum(f"a{p}", "dxbay" if s.folds else "dx", s.att_orders[p], Gather(p))

    kept = {}

    def first_back():
        gfirst = mm(v.dqkv[...], v.wqkv[...], 1, 1)
        picked = v.picked[...]
        kept["gain_one"] = jnp.sum(gfirst * (picked * rate_one), axis=0, keepdims=True)
        scaled = gfirst * one_row
        gnorm = rate_one * scaled - picked * (rate_one * rate_one * rate_one * jnp.mean(scaled * picked, axis=1, keepdims=True))
        v.gres[...] = v.gres[...] + gnorm

    def finish_rows():
        for copy in sent_mo:
            copy.wait_recv()
        picked = v.picked[...]
        branch = v.attended[...] + (v.mo_own[...] + v.mo_in[...].astype(F32)).astype(LOW).astype(F32)
        grate = live * jnp.sum(v.cotr[...].astype(F32) * branch, axis=1, keepdims=True)
        glogit = grate * gate_rate * (1.0 - gate_rate)
        router_sum = jnp.sum(glogit * picked, axis=0, keepdims=True)
        v.upd_out[...] = (route_gain * branch).astype(LOW)
        v.upd_tok[...] = (live * (v.gres[...] + glogit * router_row)).astype(LOW)
        row = iota((8, d), 0)
        gain_two_sum = gain_two_sums[0] + gain_two_sums[1]
        v.vec[0] = jnp.where(row == 0, router_sum, jnp.where(row == 1, kept["gain_one"], jnp.where(row == 2, gain_two_sum, 0.0)))
        sums["v"] = Everywhere("dxyab" if s.folds else "dx")

    tile = s.rows // 4
    writes = []

    def spread(at):
        rows = slice(at * tile, (at + 1) * tile)
        there = pl.ds(at * tile, tile)
        place = jnp.where(iota((tile, n), 0) + at * tile == wanted.astype(jnp.int32), 1.0, 0.0).astype(LOW)
        for table, update in ((v.tok, v.upd_out), (v.cot, v.upd_tok)):
            table[rows] = (table[rows].astype(F32) + mm(place, update[...])).astype(LOW)
        writes.append(pltpu.make_async_copy(v.cot.at[there], grad_tokens.at[0, there], v.local_sem.at[len(fetches) + at]))
        writes[-1].start()

    class Everywhere:
        def __init__(self, order):
            self.order, self.at = order, 0
            self.start()

        def start(self):
            self.going = send(v.vec.at[self.at], v.vec_in.at[self.at], self.order[self.at])

        def advance(self):
            self.going.wait_recv()
            v.vec[self.at + 1] = v.vec[self.at] + v.vec_in[self.at]
            self.at += 1
            if self.at < len(self.order):
                self.start()
            else:
                total = v.vec[self.at]
                if not s.folds:
                    for at, out in enumerate(o_vecs):
                        out[...] = total[at : at + 1]
                    return
                mine = iota((d, s.block), 0) == iota((d, s.block), 1) + b * s.block
                total = lax.dot_general(
                    total, jnp.where(mine, 1.0, 0.0), (((1,), (0,)), ((), ())),
                    preferred_element_type=F32, precision=lax.Precision.HIGHEST,
                )
                for at, out in enumerate(o_vecs):
                    out[...] = total[at : at + 1]

    work = {"f": feed_other, "u": other_core, "w": own_core, "r": second_back, "b": attend_back, "s": spread}
    for step in itertools.chain(*SEQUENCE):
        if step[0] in work:
            work[step[0]](int(step[1:]))
        elif step == "e0":
            first_back()
        elif step == "e1":
            finish_rows()
        elif s.folds:
            sums[step].advance()
    if not s.folds:
        for name, total in sums.items():
            total.advance()
            total.advance()
    for copy in sent:
        copy.wait_send()
    for copy in writes:
        copy.wait()


def hand_over_kernel(count, *refs):
    near, far, outs, held, sems = refs[0], refs[1:count], refs[count : 2 * count], refs[2 * count : -1], refs[-1]
    pieces = [(near, None, outs[0])]
    for src, dst, buf in zip(far, outs[1:], held, strict=True):
        cuts = 4 if src.shape[0] == 1 and src.ndim == 3 else 1
        if cuts == 1:
            pieces.append((src, buf, dst))
        else:
            rows = src.shape[1] // cuts
            pieces += [tuple(x.at[0, pl.ds(at * rows, rows)] for x in (src, buf, dst)) for at in range(cuts)]
    coming, going = {}, []
    for at, (src, buf, dst) in enumerate(pieces):
        if buf is not None:
            coming[at] = pltpu.make_async_copy(src, buf, sems.at[0, at])
            coming[at].start()
    for at, (src, buf, dst) in enumerate(pieces):
        if at in coming:
            coming[at].wait()
        going.append(pltpu.make_async_copy(src if buf is None else buf, dst, sems.at[1, at]))
        going[-1].start()
    for copy in going:
        copy.wait()


def hand_over(near, *far):
    arrays = (near, *far)
    anywhere = pl.BlockSpec(memory_space=pl.ANY)
    return pl.pallas_call(
        functools.partial(hand_over_kernel, len(arrays)),
        out_shape=[jax.ShapeDtypeStruct(x.shape, x.dtype) for x in arrays],
        in_specs=[pl.BlockSpec(memory_space=pltpu.VMEM)] + [pl.BlockSpec(memory_space=pltpu.HBM)] * len(far),
        out_specs=[anywhere] * len(arrays),
        scratch_shapes=[*[pltpu.VMEM(x.shape, x.dtype) for x in far], pltpu.SemaphoreType.DMA((2, len(arrays) + 3))],
        compiler_params=pltpu.CompilerParams(vmem_limit_bytes=16 * 2**20),
        name="hand_over",
    )(pltpu.with_memory_space_constraint(near, pltpu.VMEM), *(pltpu.with_memory_space_constraint(x, pltpu.HBM) for x in far))


def local(tokens, key_mask, lengths, routed, w_router, gain_one, gain_two, w_qkv, w_out, w_up, w_down, cotangent):
    _, rows, d = tokens.shape
    n, f = routed.shape[1], w_up.shape[1]
    batch = lax.axis_size("batch")
    s = Sizes(rows, d, n, f, batch)
    found = scratch_of(s)
    vmem, smem, anywhere = (pl.BlockSpec(memory_space=space) for space in (pltpu.VMEM, pltpu.SMEM, pl.ANY))
    def f32(*shape):
        return jax.ShapeDtypeStruct(shape, F32)

    piece = s.block if s.folds else d
    block_out, grad_tokens, g_up, g_down, g_qkv, g_out, *g_vecs = pl.pallas_call(
        functools.partial(layer_kernel, s, tuple(found)),
        out_shape=(
            pltpu.VMEM(tokens.shape, LOW),
            jax.ShapeDtypeStruct(tokens.shape, LOW),
            f32(piece, f),
            f32(piece, f),
            f32(piece, 3 * d) if s.folds else f32(s.pairs, d, s.pair),
            f32(piece, d),
            *[f32(1, piece)] * 3,
        ),
        in_specs=[anywhere, anywhere, vmem, smem, vmem, vmem, vmem, vmem, anywhere, anywhere, anywhere, anywhere],
        out_specs=[vmem, anywhere] + [vmem] * 7,
        scratch_shapes=list(found.values()),
        compiler_params=pltpu.CompilerParams(collective_id=0, has_side_effects=True, vmem_limit_bytes=VMEM_BYTES),
        name="layer",
    )(
        tokens, cotangent, key_mask, lengths, routed, w_router, gain_one, gain_two, w_qkv, w_out, w_up, w_down,
    )
    if not s.folds:
        g_up, g_down, *g_vecs = (lax.psum_scatter(g, "batch", scatter_dimension=g.ndim - 1 if g.shape[0] == 1 else 0, tiled=True) for g in (g_up, g_down, *g_vecs))
        att = lax.psum_scatter(g_qkv, "batch", scatter_dimension=1, tiled=True).astype(LOW)
        att = lax.all_gather(att, "mp", axis=0).astype(F32)
        att = jnp.transpose(att, (2, 0, 1, 3)).reshape(s.block, 4 * d)
        g_qkv, g_out = att[:, : 3 * d], att[:, 3 * d :]
    block_out, grad_tokens, g_up, g_down, g_qkv, g_out, *g_vecs = hand_over(
        block_out, grad_tokens, g_up, g_down, g_qkv, g_out, *g_vecs
    )
    g_router, g_one, g_two = (g.reshape(s.block) for g in g_vecs)
    return block_out, grad_tokens, g_router, g_one, g_two, g_qkv, g_out, g_up, g_down.T


def solution(mesh):
    rows_spec = P(("batch", "mp"), None, None)
    in_specs = (
        rows_spec,
        P(("batch", "mp"), None),
        P(("batch", "mp")),
        P(("batch", "mp"), None),
        P(),
        P(),
        P(),
        P(),
        P(),
        P(None, "mp"),
        P("mp", None),
        rows_spec,
    )
    out_specs = (
        rows_spec,
        rows_spec,
        P("batch"),
        P("batch"),
        P("batch"),
        P("batch", None),
        P("batch", None),
        P("batch", "mp"),
        P("mp", "batch"),
    )
    return jax.shard_map(local, mesh=mesh, in_specs=in_specs, out_specs=out_specs, check_vma=False)
```

time: 123 us -> 90.4 us (0.73)
  Pallas kernels: 115 us -> 88.7 us
  local copies, waits for them, and re-layouts: 6.97 us -> 0 us
    pallas_call x1, Pallas kernels: 106 us -> 83.3 us  [local(): pl.pallas_call(functools.partial(layer_kernel, s, tuple(found)), out_shap...]
    reshape x3 -> x0, local copies, waits for them, and re-layouts: 3.79 us -> none  [the longest x1 1.26 us: local(): w_router.reshape(1, d)]
    pallas_call x1, Pallas kernels: 8.48 us -> 5.33 us  [hand_over(): pl.pallas_call(functools.partial(hand_over_kernel, len(arrays)), out_shap...]
    unnamed x1 -> x0, local copies, waits for them, and re-layouts: 1.87 us -> none
    squeeze x1 -> x0, local copies, waits for them, and re-layouts: 1.32 us -> none  [local(): g_vec[2]]
where the time goes in v2:
time: 90.4 us; the launch traced here: 90.1 us
  Pallas kernels  88.7 us (98%)
  between operations  1.48 us (2%)
    pallas_call x1, Pallas kernels, local(): pl.pallas_call(functools.partial(layer_kernel, s, tuple(found)), out_shap...  83.3 us
    pallas_call x1, Pallas kernels, hand_over(): pl.pallas_call(functools.partial(hand_over_kernel, len(arrays)), out_shap...  5.33 us

profile of v2, /device:TPU:0, one launch (start us, length us, event | category | flops | bytes accessed | tf_op | source)
XLA Modules:
  0.0 90.1 jit_solution(12592492741204830608)
XLA Ops:
  1.3 83.3 %layer.1 = (bf16[1,2048,768]{2,1,0:T(8,128)(2,1)S(1)}, bf16[1,2048,768]{2,1,0:T(8,128)(2,1)}, f32[96,768]{1,0:T(8,128)}, f32[96,768]{1,0:T(8,128)}, f32[96,2304]...) custom-call(bf16[1,2048,768]{2,1,0:T(8,128)(2,1)} %refs_0_.1, ...), custom_call_target="tpu_custom_call" | custom-call | tf_op jit(solution)/shard_map/layer/pallas_call | solution.py:556
  84.6 5.3 %hand_over.1 = (bf16[1,2048,768]{2,1,0:T(8,128)(2,1)}, bf16[1,2048,768]{2,1,0:T(8,128)(2,1)}, f32[96,768]{1,0:T(8,128)}, f32[96,768]{1,0:T(8,128)}, f32[96,2304]...) custom-call(bf16[1,2048,768]{2,1,0:T(8,128)(2,1)S(1)} %get-tuple-element.27.refs_0_, ...), custom_call_target="tpu_custom_call" | custom-call | tf_op jit(solution)/shard_map/hand_over/pallas_call | solution.py:534

commit v3 on v2

v3 whole, which is shorter than its diff:
```python
import functools
import itertools
import types

import jax
import jax.numpy as jnp
from jax import lax
from jax.experimental import pallas as pl
from jax.experimental.pallas import tpu as pltpu
from jax.sharding import PartitionSpec as P

HEADS = 12
EPSILON = 1e-06
LOW = jnp.bfloat16
F32 = jnp.float32
MESH = pl.DeviceIdType.MESH
VMEM_BYTES = 58 * 2**20
AXES = "dxbay"
MLP_ORDERS = ("yab", "aby", "yab", "yab", "aby", "yab")
ATT_ORDERS = ("dxyab", "dxyab", "dxaby", "dyxabG", "dxyabG", "daxyb")
SEQUENCE = (
    ("f0", "f1", "u0", "u1", "u2", "u3", "u4", "u5", "w0", "w1", "w2", "w3", "w4", "t", "r0", "r1", "w5"),
    ("r2", "r3", "b0", "m1", "b1", "m0", "a0", "b2", "a1", "b3", "m4", "a2", "m2", "b4", "a3", "o0", "b5"),
    ("a4", "m0", "e0", "m1", "a5", "a0", "m3", "e1", "m2", "m4", "m5", "a1", "m0", "a3", "a5", "a2", "o1"),
    ("m3", "z", "m1", "s0", "s1", "a4", "v", "m2", "a0", "m5", "s2", "s3", "m4", "a3", "s4", "s5", "a2", "s6"),
    ("s7", "a5", "a1", "v", "a0", "m3", "a4", "a3", "m5", "a5", "v", "a1", "a2", "a4", "a0", "a3", "v", "a5"),
    ("a2", "a1", "a0", "a4", "a0", "a3", "a5", "a2", "v", "a1", "a5", "a2", "a1", "a4"),
)


def mm(a, b, along_a=1, along_b=0):
    return lax.dot_general(a, b, (((along_a,), (along_b,)), ((), ())), preferred_element_type=F32)


def norm_rate(v):
    return lax.rsqrt(jnp.mean(v * v, axis=1, keepdims=True) + EPSILON)


def gelu_and_slope(v):
    c = 0.7978845608028654
    square = v * v
    t = jnp.tanh(v * (c + (c * 0.044715) * square))
    half = 0.5 + 0.5 * t
    slope = half + (0.5 * v) * (1.0 - t * t) * (c + (c * 3 * 0.044715) * square)
    return v * half, slope


def iota(shape, dim):
    return lax.broadcasted_iota(jnp.int32, shape, dim)


class Sizes:
    def __init__(self, rows, width, slots, hidden, batch):
        self.rows, self.width, self.slots, self.hidden, self.batch = rows, width, slots, hidden, batch
        self.block = width // batch
        self.folds = batch == 8 and self.block % 16 == 0
        self.pair = 2 * (width // HEADS)
        self.pairs = HEADS // 2
        self.part = hidden // 3
        self.half, self.work = slots // 2, slots * 3 // 4
        self.spill = slots - self.work
        self.mlp_orders = MLP_ORDERS if self.folds else ("",) * len(MLP_ORDERS)
        self.att_orders = ATT_ORDERS if self.folds else ("dx",) * len(ATT_ORDERS)
        self.tail = (self.block,) if self.folds else (width,)

    def table(self, axes, columns):
        return (*(2 for axis in AXES if axis in axes), *self.tail, columns)


def scratch_of(s):
    n, d, f = s.slots, s.width, s.hidden
    found = dict(
        cot=pltpu.VMEM((s.rows, d), LOW),
        wqkv=pltpu.VMEM((d, 3 * d), LOW),
        wout=pltpu.VMEM((d, d), LOW),
        wup=pltpu.VMEM((2, d, f), LOW),
        wdn=pltpu.VMEM((2, f, d), LOW),
        wout_t=pltpu.VMEM((d, d), LOW),
        wup_t=pltpu.VMEM((2, f, d), LOW),
        wdn_t=pltpu.VMEM((2, d, f), LOW),
        pick=pltpu.VMEM((n, s.rows), LOW),
        picked=pltpu.VMEM((n, d), F32),
        cotr=pltpu.VMEM((n, d), LOW),
        first=pltpu.VMEM((n, d), LOW),
        qkv=pltpu.VMEM((n, 3 * d), LOW),
        bias=pltpu.VMEM((n, n), F32),
        probs=pltpu.VMEM((HEADS, n, n), LOW),
        mixed=pltpu.VMEM((n, d), LOW),
        first_t=pltpu.VMEM((d, n), LOW),
        mixed_t=pltpu.VMEM((d, n), LOW),
        sec_t=pltpu.VMEM((d, 2 * s.work), LOW),
        gm_t=pltpu.VMEM((d, 2 * s.work), LOW),
        upd_out=pltpu.VMEM((n, d), LOW),
        upd_tok=pltpu.VMEM((n, d), LOW),
        attended=pltpu.VMEM((n, d), F32),
        resid=pltpu.VMEM((n, d), F32),
        sec=pltpu.VMEM((2 * s.work, d), LOW),
        gm=pltpu.VMEM((2 * s.work, d), LOW),
        act=pltpu.VMEM((2, 2 * s.work, f), LOW),
        gpre=pltpu.VMEM((2, 2 * s.work, f), LOW),
        gs_own=pltpu.VMEM((s.work, d), F32),
        mo_own=pltpu.VMEM((s.work, d), F32),
        gs_out=pltpu.VMEM((s.work, d), LOW),
        mo_out=pltpu.VMEM((s.work, d), LOW),
        gs_in=pltpu.VMEM((s.work, d), LOW),
        mo_in=pltpu.VMEM((s.work, d), LOW),
        spill_out=pltpu.VMEM((4, s.spill, d), LOW),
        spill_in=pltpu.VMEM((5, s.spill, d), LOW),
        mo=pltpu.VMEM((n, d), F32),
        mask_row=pltpu.VMEM((1, s.rows), jnp.int32),
        wanted_row=pltpu.VMEM((1, n), jnp.int32),
        gres=pltpu.VMEM((n, d), F32),
        gatt=pltpu.VMEM((n, d), LOW),
        gmix=pltpu.VMEM((n, d), LOW),
        dqkv=pltpu.VMEM((n, 3 * d), LOW),
        vec=pltpu.VMEM((6, 8, d), F32),
        vec_in=pltpu.VMEM((5, 8, d), F32),
        send_sem=pltpu.SemaphoreType.DMA((112,)),
        recv_sem=pltpu.SemaphoreType.DMA((112,)),
        summed=pltpu.VMEM((2, *s.tail, f), F32),
        router=pltpu.VMEM((d,), LOW),
        one=pltpu.VMEM((d,), LOW),
        two=pltpu.VMEM((d,), LOW),
        write_sem=pltpu.SemaphoreType.DMA((12,)),
        local_sem=pltpu.SemaphoreType.DMA((24,)),
    )
    batch_axes = "bay" if s.folds else ""
    for name, orders, axes, columns in (("m", s.mlp_orders, batch_axes, s.part), ("a", s.att_orders, "dx" + batch_axes, s.pair)):
        for at, order in enumerate(orders):
            left = axes
            found[f"{name}{at}_0"] = pltpu.VMEM(s.table(left, columns), LOW)
            for step, axis in enumerate(order.strip("G")):
                left = left.replace(axis, "")
                found[f"{name}{at}_{step + 1}"] = pltpu.VMEM(s.table(left, columns), LOW)
            if name == "m":
                found[f"u{at}"] = pltpu.VMEM(s.table(axes, columns), LOW)
    if s.folds:
        found["gathered"] = pltpu.VMEM((4, s.pairs, s.block, s.pair), LOW)
    return found


def layer_kernel(s, names, *refs):
    ins, outs, scratch = refs[:12], refs[12:17], refs[17:]
    tokens, cotangent, key_mask, lengths, routed, w_router, gain_one, gain_two, w_qkv, w_out, w_up, w_down = ins
    block_out, o_att, o_vec, grad_tokens, o_mlp = outs
    v = types.SimpleNamespace(**dict(zip(names, scratch, strict=True)), tok=block_out.at[0])
    n, d, f, pair = s.slots, s.width, s.hidden, s.pair
    half_rows = n // 2

    b, m = lax.axis_index("batch"), lax.axis_index("mp")
    lo, hi = m % 2, m // 2
    y = b % 2
    here = {"d": lo, "x": hi, "y": y}
    other_m = {"d": m + 1 - 2 * lo, "x": m + 2 - 4 * hi, "f": 3 - m}
    peer = {axis: (b, to) for axis, to in other_m.items()} | {"y": (b + 1 - 2 * y, m), "q": (b + 1 - 2 * y, other_m["x"])}
    if s.folds:
        zl, zh = (b // 2) % 2, b // 4
        here |= {"a": zl, "b": zh}
        peer |= {"a": (b + 2 - 4 * zl, m), "b": (b + 4 - 8 * zh, m)}

    barrier = pltpu.get_barrier_semaphore()
    for other in peer.values():
        pl.semaphore_signal(barrier, inc=1, device_id=other, device_id_type=MESH)

    sent = []

    def send(src, dst, axis):
        at = len(sent)
        copy = pltpu.make_async_remote_copy(
            src_ref=src,
            dst_ref=dst,
            send_sem=v.send_sem.at[at],
            recv_sem=v.recv_sem.at[at],
            device_id=peer[axis],
            device_id_type=MESH,
        )
        copy.start()
        sent.append(copy)
        return copy

    fetches = []

    def fetch(src, dst):
        fetches.append(pltpu.make_async_copy(src, dst, v.local_sem.at[len(fetches)]))
        fetches[-1].start()
        return fetches[-1]

    writes, stored = [], []

    def write(src, dst):
        writes.append(pltpu.make_async_copy(src, dst, v.write_sem.at[len(writes)]))
        writes[-1].start()

    quarter = s.rows // 4
    quarters = [pl.ds(at * quarter, quarter) for at in range(4)]
    got_wanted = fetch(routed, v.wanted_row)
    got_rows = [fetch(src, dst) for src, dst in ((w_router, v.router), (gain_one, v.one), (gain_two, v.two))]
    got_tok = [fetch(tokens.at[0, there], v.tok.at[there]) for there in quarters]
    got_cot = [fetch(cotangent.at[0, there], v.cot.at[there]) for there in quarters]
    got_mask = fetch(key_mask, v.mask_row)

    got_wanted.wait()
    live_count = lengths[0] // 8
    wanted = jnp.where(iota((1, n), 1) < live_count, v.wanted_row[...], -1).astype(F32)
    on_diagonal = iota((n, n), 0) == iota((n, n), 1)
    wanted_column = jnp.sum(jnp.where(on_diagonal, wanted, 0.0), axis=1, keepdims=True).astype(jnp.int32)
    live = jnp.where(iota((n, 1), 0) < live_count, 1.0, 0.0)
    v.pick[...] = jnp.where(iota((n, s.rows), 1) == wanted_column, 1.0, 0.0).astype(LOW)

    def gather(table, got):
        total = 0.0
        for at in range(4):
            got[at].wait()
            cols = slice(at * quarter, (at + 1) * quarter)
            total = total + mm(v.pick[:, cols], table[cols])
        return total

    picked = gather(v.tok, got_tok)
    v.picked[...] = picked
    for got in got_rows:
        got.wait()
    router_row, one_row, two_row = (row[...].astype(F32).reshape(1, d) for row in (v.router, v.one, v.two))
    gate_rate = 1.0 / (1.0 + jnp.exp(-jnp.sum(picked * router_row, axis=1, keepdims=True)))
    route_gain = live * gate_rate

    got_qkv = fetch(w_qkv, v.wqkv)
    cot_rows = gather(v.cot, got_cot)
    got_out = fetch(w_out, v.wout)
    got_up = fetch(w_up, v.wup.at[0])
    got_down = fetch(w_down, v.wdn.at[0])
    half, work, spill = s.half, s.work, s.spill
    mine_a, other_a = pl.ds(0, half), pl.ds(half, half)
    mine_b, other_b = pl.ds(2 * half, spill), pl.ds(2 * half + spill, spill)
    gm = (route_gain * cot_rows).astype(LOW)
    v.gm[0:half] = gm[:half]
    v.spill_out[0] = gm[work:]

    pl.semaphore_wait(barrier, len(peer))
    sent_gm = [send(v.gm.at[mine_a], v.gm.at[other_a], "x")]
    spilt_gm = send(v.spill_out.at[0], v.spill_in.at[0], "y")
    sent_up = send(w_up, v.wup.at[1], "d")
    sent_down = send(w_down, v.wdn.at[1], "d")

    v.cotr[...] = cot_rows.astype(LOW)
    rate_one = norm_rate(picked)
    v.first[...] = (picked * rate_one * one_row).astype(LOW)
    got_qkv.wait()
    for at in range(0, 3 * d, 256):
        v.qkv[:, at : at + 256] = mm(v.first[...], v.wqkv[:, at : at + 256]).astype(LOW)

    place_spill = jnp.where(iota((spill, spill), 0) + half - live_count == iota((spill, spill), 1), 1.0, 0.0).astype(LOW)
    live_b = live[half:work]

    def merge(own, arrived):
        return (own.astype(F32) * live_b + mm(place_spill, arrived)).astype(LOW)

    def part_back(merged):
        return mm(place_spill, merged, 0, 0).astype(LOW)

    peer_live = 2 * work - live_count
    place_peer = jnp.where(iota((spill, spill), 0) + half - peer_live == iota((spill, spill), 1), 1.0, 0.0).astype(LOW)

    spilt_gm.wait_recv()
    v.gm[2 * half : 2 * half + spill] = merge(gm[half:work], v.spill_in[0])
    sent_gm.append(send(v.gm.at[mine_b], v.gm.at[other_b], "x"))

    got_mask.wait()
    mask_rows = jnp.broadcast_to(v.mask_row[...].astype(F32), (8, s.rows)).astype(LOW)
    key_open = mm(mask_rows, v.pick[...], 1, 1)[0:1] > 0.5
    earlier = iota((n, n), 1) < iota((n, n), 0)
    v.bias[...] = jnp.where((earlier & key_open) | on_diagonal, 0.0, -1e30)

    lane = iota((n, pair), 1)
    side = [lane < pair // 2, lane >= pair // 2]

    def only(x, at):
        return jnp.where(side[at], x.astype(F32), 0.0).astype(LOW)

    for p in range(s.pairs):
        q, k, val = (v.qkv[:, g * d + p * pair : g * d + (p + 1) * pair] for g in range(3))
        q = (q.astype(F32) * (d // HEADS) ** -0.5).astype(LOW)
        total = 0.0
        for h in range(2):
            scores = mm(only(q, h), k, 1, 1) + v.bias[...]
            powers = jnp.exp(scores - jnp.max(scores, axis=1, keepdims=True))
            probs = (powers * (1.0 / jnp.sum(powers, axis=1, keepdims=True))).astype(LOW)
            v.probs[2 * p + h] = probs
            total = total + mm(probs, only(val, h))
        v.mixed[:, p * pair : (p + 1) * pair] = total.astype(LOW)

    got_out.wait()

    def second(start, stop):
        rows = slice(start, stop)
        attended = mm(v.mixed[rows], v.wout[...])
        v.attended[rows] = attended
        resid = v.picked[rows] + attended
        v.resid[rows] = resid
        return (resid * norm_rate(resid) * two_row).astype(LOW)

    normed = second(0, n)
    v.spill_out[1] = normed[work:]
    spilt_sec = send(v.spill_out.at[1], v.spill_in.at[1], "y")
    v.sec[0:half] = normed[:half]
    sent_sec = [send(v.sec.at[mine_a], v.sec.at[other_a], "x")]
    second_b = normed[half:work]

    def feed(start, count):
        rows = slice(start, start + count)
        x, g = v.sec[rows], v.gm[rows]
        gs = 0.0
        for w in range(2):
            act, slope = gelu_and_slope(mm(x, v.wup[w]))
            v.act[w, rows] = act.astype(LOW)
            gpre = (mm(g, v.wdn_t[w]) * slope).astype(LOW)
            v.gpre[w, rows] = gpre
            gs = gs + mm(gpre, v.wup_t[w])
        return gs

    def feed_out(start, count):
        rows = slice(start, start + count)
        return mm(v.act[0, rows], v.wdn[0]) + mm(v.act[1, rows], v.wdn[1])

    got_up.wait()
    got_down.wait()
    sent_up.wait_recv()
    sent_down.wait_recv()
    for w in range(2):
        v.wup_t[w] = v.wup[w].T
        v.wdn_t[w] = v.wdn[w].T
    v.gs_own[0:half] = feed(0, half)
    spilt_sec.wait_recv()
    v.sec[2 * half : 2 * half + spill] = merge(second_b, v.spill_in[1])
    sent_sec.append(send(v.sec.at[mine_b], v.sec.at[other_b], "x"))
    gs = feed(2 * half, spill)
    v.gs_own[half:work] = gs
    v.spill_out[2] = gs.astype(LOW)
    spilt_own = send(v.spill_out.at[2], v.spill_in.at[2], "y")
    v.mo_own[0:half] = feed_out(0, half)
    v.mo_own[half:work] = feed_out(2 * half, spill)
    v.sec_t[:, :half] = v.sec[0:half].T
    v.gm_t[:, :half] = v.gm[0:half].T
    for copy in sent_gm:
        copy.wait_recv()
    v.gm_t[:, half:] = v.gm[half:].T
    sent_gs, sent_mo, spilt = [], [], {}

    def transposes():
        v.wout_t[...] = v.wout[...].T
        v.first_t[...] = v.first[...].T
        v.mixed_t[...] = v.mixed[...].T

    def send_back(out, into, start, count):
        there = pl.ds(start, count)
        return send(out.at[there], into.at[there], "x")

    def feed_other(at):
        sent_sec[at].wait_recv()
        start, count, into = (half, half, 0) if at == 0 else (2 * half + spill, spill, half)
        rows = slice(into, into + count)
        v.gs_out[rows] = feed(start, count).astype(LOW)
        if at == 0:
            sent_gs.append(send_back(v.gs_out, v.gs_in, 0, half // 2))
        else:
            sent_gs.append(send_back(v.gs_out, v.gs_in, half, spill))
            spilt["gs"] = send(v.gs_out.at[pl.ds(half, spill)], v.spill_in.at[4], "q")
            sent_gs.append(send_back(v.gs_out, v.gs_in, half // 2, half // 2))
        v.mo_out[rows] = feed_out(start, count).astype(LOW)
        if at == 1:
            sent_mo.append(send_back(v.mo_out, v.mo_in, half, spill))
            sent_mo.append(send_back(v.mo_out, v.mo_in, 0, half))
            v.sec_t[:, half:] = v.sec[half:].T

    def weight_grad(at, w):
        left, right = (v.sec_t, v.gpre) if at < 3 else (v.gm_t, v.act)
        cols = slice(at % 3 * s.part, (at % 3 + 1) * s.part)
        return mm(left[...], right[w, :, cols])

    sent_core = []

    def other_core(at):
        table = getattr(v, f"u{at}")
        table[...] = weight_grad(at, 1).astype(LOW).reshape(table.shape)
        sent_core.append(send(table, getattr(v, f"m{at}_0"), "d"))

    class Sum:
        def __init__(self, name, axes, order, finish):
            self.name, self.axes, self.order, self.finish, self.at = name, axes, order, finish, 0
            if order:
                self.start()

        def table(self, at):
            return getattr(v, f"{self.name}_{at}")

        def start(self):
            axis = self.order[self.at]
            src = self.table(self.at).at[tuple(1 - here[k] if k == axis else slice(None) for k in self.axes)]
            self.going = send(src, self.table(self.at + 1), axis)

        def advance(self):
            if self.at == len(self.order):
                self.finish.advance()
                return
            axis = self.order[self.at]
            self.going.wait_recv()
            kept, arrived = self.table(self.at), self.table(self.at + 1)
            last = self.at + 1 == len(self.order)
            rest = self.axes.replace(axis, "")
            for index in itertools.product(*[range(2)] * len(rest)):
                full = dict(zip(rest, index, strict=True)) | {axis: here[axis]}
                total = arrived[index].astype(F32) + kept[tuple(full[k] for k in self.axes)].astype(F32)
                if last:
                    self.finish.begin(total)
                else:
                    arrived[index] = total.astype(LOW)
            self.axes, self.at = rest, self.at + 1
            if not last:
                self.start()

    class Store:
        def __init__(self, at):
            self.at = at

        def begin(self, total):
            kind, cols = self.at // 3, slice(self.at % 3 * s.part, (self.at % 3 + 1) * s.part)
            v.summed[kind, :, cols] = total
            stored.append(self.at)
            if all(3 * kind + at in stored for at in range(3)):
                write(v.summed.at[kind], o_mlp.at[kind])

    class Gather:
        def __init__(self, p, direct):
            self.p, self.direct = p, direct

        def begin(self, total):
            if not s.folds:
                o_att[self.p] = total
                return
            piece = v.gathered.at[m, self.p]
            piece[...] = total.astype(LOW)
            self.over_x = send(piece, piece, "x")
            self.others = [send(piece, piece, "d")]
            if self.direct:
                self.others.append(send(piece, piece, "f"))
            self.handed_on = self.direct

        def advance(self):
            if not self.handed_on:
                self.over_x.wait_recv()
                piece = v.gathered.at[other_m["x"], self.p]
                self.others.append(send(piece, piece, "d"))
                self.handed_on = True
                return
            if self.direct:
                self.over_x.wait_recv()
            for copy in self.others:
                copy.wait_recv()
            for g in range(4):
                o_att[g, self.p] = v.gathered[g, self.p]

    sums = {}

    def own_core(at):
        own = weight_grad(at, 0)
        sent_core[at].wait_recv()
        table = getattr(v, f"m{at}_0")
        table[...] = (table[...].astype(F32) + own.reshape(table.shape)).astype(LOW)
        if s.folds:
            sums[f"m{at}"] = Sum(f"m{at}", "bay", s.mlp_orders[at], Store(at))
        else:
            v.summed[at // 3, :, at % 3 * s.part : (at % 3 + 1) * s.part] = table[...].astype(F32)
            if at % 3 == 2:
                write(v.summed.at[at // 3], o_mlp.at[at // 3])

    gain_two_sums = []

    def second_back(at):
        if at < 3:
            start, stop = ((0, half // 2), (half, work), (half // 2, half))[at]
            sent_gs[at].wait_recv()
            gs = (v.gs_own[start:stop] + v.gs_in[start:stop].astype(F32)).astype(LOW)
            if at == 1:
                gs = gs.astype(F32) * live_b
        else:
            start, stop = work, n
            spilt_own.wait_recv()
            spilt["gs"].wait_recv()
            gs = mm(place_peer, (v.spill_in[2].astype(F32) + v.spill_in[4].astype(F32)).astype(LOW), 0, 0)
        rows = slice(start, stop)
        gs = gs.astype(F32)
        resid = v.resid[rows]
        rate = norm_rate(resid)
        gain_two_sums.append(jnp.sum(gs * (resid * rate), axis=0, keepdims=True))
        scaled = gs * two_row
        gres = rate * scaled - resid * (rate * rate * rate * jnp.mean(scaled * resid, axis=1, keepdims=True))
        v.gres[rows] = gres
        gatt = (route_gain[rows] * v.cotr[rows].astype(F32) + gres).astype(LOW)
        v.gatt[rows] = gatt
        v.gmix[rows] = mm(gatt, v.wout_t[...]).astype(LOW)

    def part_mo(at):
        if at == 0:
            sent_mo[0].wait_recv()
            mo = (v.mo_own[half:work] + v.mo_in[half:work].astype(F32)).astype(LOW)
            v.spill_out[3] = part_back(mo)
            spilt["mo"] = send(v.spill_out.at[3], v.spill_in.at[3], "y")
            v.mo[half:work] = mo.astype(F32)
        else:
            sent_mo[1].wait_recv()
            v.mo[0:half] = (v.mo_own[0:half] + v.mo_in[0:half].astype(F32)).astype(LOW).astype(F32)
            spilt["mo"].wait_recv()
            v.mo[work:n] = v.spill_in[3].astype(F32)

    def attend_back(p):
        where = [slice(g * d + p * pair, g * d + (p + 1) * pair) for g in range(3)]
        q, k, val = (v.qkv[:, cols] for cols in where)
        gmix = v.gmix[:, p * pair : (p + 1) * pair]
        gq, gk, gv = 0.0, 0.0, 0.0
        for h in range(2):
            probs = v.probs[2 * p + h]
            gmix_h = only(gmix, h)
            gprobs = mm(gmix_h, val, 1, 1)
            wide = probs.astype(F32)
            product = gprobs * wide
            gscores = product - wide * jnp.sum(product, axis=1, keepdims=True)
            gscores = (gscores * (d // HEADS) ** -0.5).astype(LOW)
            gq = gq + mm(gscores, only(k, h))
            gk = gk + mm(gscores, only(q, h), 0, 0)
            gv = gv + mm(probs, gmix_h, 0, 0)
        table = getattr(v, f"a{p}_0")
        lower = []
        for cols, grad in zip(where, (gq, gk, gv), strict=True):
            lower.append(grad.astype(LOW))
            v.dqkv[:, cols] = lower[-1]
        both = mm(v.first_t[...], jnp.concatenate(lower[:2], axis=1)).astype(LOW)
        shape = table.shape[2:]
        table[0, 0] = both[:, :pair].reshape(shape)
        table[1, 0] = both[:, pair:].reshape(shape)
        table[0, 1] = mm(v.first_t[...], lower[2]).astype(LOW).reshape(shape)
        table[1, 1] = mm(v.mixed_t[...], v.gatt[:, p * pair : (p + 1) * pair]).astype(LOW).reshape(shape)
        order = s.att_orders[p]
        sums[f"a{p}"] = Sum(f"a{p}", "dxbay" if s.folds else "dx", order.strip("G"), Gather(p, "G" in order))

    kept = {}

    def first_back(at):
        rows = slice(at * half, (at + 1) * half)
        gfirst = mm(v.dqkv[rows], v.wqkv[...], 1, 1)
        picked, rate = v.picked[rows], rate_one[rows]
        kept[at] = jnp.sum(gfirst * (picked * rate), axis=0, keepdims=True)
        scaled = gfirst * one_row
        gnorm = rate * scaled - picked * (rate * rate * rate * jnp.mean(scaled * picked, axis=1, keepdims=True))
        v.gres[rows] = v.gres[rows] + gnorm

    def finish_rows():
        picked = v.picked[...]
        branch = v.attended[...] + v.mo[...]
        grate = live * jnp.sum(v.cotr[...].astype(F32) * branch, axis=1, keepdims=True)
        glogit = grate * gate_rate * (1.0 - gate_rate)
        router_sum = jnp.sum(glogit * picked, axis=0, keepdims=True)
        v.upd_out[...] = (route_gain * branch).astype(LOW)
        v.upd_tok[...] = (live * (v.gres[...] + glogit * router_row)).astype(LOW)
        row = iota((8, d), 0)
        gain_two_sum = sum(gain_two_sums)
        v.vec[0] = jnp.where(row == 0, router_sum, jnp.where(row == 1, kept[0] + kept[1], jnp.where(row == 2, gain_two_sum, 0.0)))
        sums["v"] = Everywhere("dxyab" if s.folds else "dx")

    tile = s.rows // 8

    def spread(at):
        rows = slice(at * tile, (at + 1) * tile)
        there = pl.ds(at * tile, tile)
        place = jnp.where(iota((tile, n), 0) + at * tile == wanted.astype(jnp.int32), 1.0, 0.0).astype(LOW)
        for table, update in ((v.tok, v.upd_out), (v.cot, v.upd_tok)):
            table[rows] = (table[rows].astype(F32) + mm(place, update[...])).astype(LOW)
        write(v.cot.at[there], grad_tokens.at[0, there])

    class Everywhere:
        def __init__(self, order):
            self.order, self.at = order, 0
            self.start()

        def start(self):
            self.going = send(v.vec.at[self.at], v.vec_in.at[self.at], self.order[self.at])

        def advance(self):
            self.going.wait_recv()
            v.vec[self.at + 1] = v.vec[self.at] + v.vec_in[self.at]
            self.at += 1
            if self.at < len(self.order):
                self.start()
            else:
                total = v.vec[self.at]
                if not s.folds:
                    o_vec[...] = total
                    return
                mine = iota((d, s.block), 0) == iota((d, s.block), 1) + b * s.block
                o_vec[...] = lax.dot_general(
                    total, jnp.where(mine, 1.0, 0.0), (((1,), (0,)), ((), ())),
                    preferred_element_type=F32, precision=lax.Precision.HIGHEST,
                )

    steps = {"f": feed_other, "u": other_core, "w": own_core, "r": second_back, "b": attend_back, "s": spread, "o": part_mo, "e": first_back}
    for step in itertools.chain(*SEQUENCE):
        if step[0] in steps:
            steps[step[0]](int(step[1:]))
        elif step == "t":
            transposes()
        elif step == "z":
            finish_rows()
        elif s.folds:
            sums[step].advance()
    if not s.folds:
        for name, total in sums.items():
            total.advance()
            total.advance()
    for copy in sent:
        copy.wait_send()
    for copy in writes:
        copy.wait()


def hand_over_kernel(block_out, att, vec, grad_tokens, mlp, out, tok, g_up, g_down, g_qkv, g_out, *rest):
    *vecs, tok_buf, mlp_buf, qkv_buf, out_buf, come_sem, go_sem = rest
    _, pairs, _, pair = att.shape
    d = g_out.shape[1]
    rows = tok.shape[1] // 4
    going = []

    def go(src, dst):
        going.append(pltpu.make_async_copy(src, dst, go_sem.at[len(going)]))
        going[-1].start()

    coming = []
    for src, dst in (
        *[(grad_tokens.at[0, pl.ds(at * rows, rows)], tok_buf.at[pl.ds(at * rows, rows)]) for at in range(4)],
        *[(mlp.at[at], mlp_buf.at[at]) for at in range(2)],
    ):
        coming.append(pltpu.make_async_copy(src, dst, come_sem.at[len(coming)]))
        coming[-1].start()
    go(block_out, out)
    for p in range(pairs):
        for g in range(3):
            qkv_buf[:, g * d + p * pair : g * d + (p + 1) * pair] = att[g, p].astype(F32)
        out_buf[:, p * pair : (p + 1) * pair] = att[3, p].astype(F32)
    go(qkv_buf, g_qkv)
    go(out_buf, g_out)
    for at, row in enumerate(vecs):
        row[...] = vec[at : at + 1]
    for at in range(4):
        coming[at].wait()
        there = pl.ds(at * rows, rows)
        go(tok_buf.at[there], tok.at[0, there])
    for at, dst in enumerate((g_up, g_down)):
        coming[4 + at].wait()
        go(mlp_buf.at[at], dst)
    for copy in going:
        copy.wait()


def hand_over(block_out, att, vec, grad_tokens, mlp):
    _, block, f = mlp.shape
    _, rows, d = block_out.shape
    vmem, hbm, anywhere = (pl.BlockSpec(memory_space=space) for space in (pltpu.VMEM, pltpu.HBM, pl.ANY))
    near = [pltpu.with_memory_space_constraint(x, pltpu.VMEM) for x in (block_out, att, vec)]
    far = [pltpu.with_memory_space_constraint(x, pltpu.HBM) for x in (grad_tokens, mlp)]
    shapes = [((block, f), F32), ((block, f), F32), ((block, 3 * d), F32), ((block, d), F32)]
    return pl.pallas_call(
        hand_over_kernel,
        out_shape=[
            *[jax.ShapeDtypeStruct(block_out.shape, LOW)] * 2,
            *[jax.ShapeDtypeStruct(shape, dtype) for shape, dtype in shapes],
            *[jax.ShapeDtypeStruct((1, block), F32)] * 3,
        ],
        in_specs=[vmem] * 3 + [hbm] * 2,
        out_specs=[anywhere] * 6 + [vmem] * 3,
        scratch_shapes=[
            pltpu.VMEM((rows, d), LOW),
            pltpu.VMEM(mlp.shape, F32),
            *[pltpu.VMEM(shape, dtype) for shape, dtype in shapes[2:]],
            pltpu.SemaphoreType.DMA((6,)),
            pltpu.SemaphoreType.DMA((9,)),
        ],
        compiler_params=pltpu.CompilerParams(vmem_limit_bytes=16 * 2**20),
        name="hand_over",
    )(*near, *far)


def local(tokens, key_mask, lengths, routed, w_router, gain_one, gain_two, w_qkv, w_out, w_up, w_down, cotangent):
    _, rows, d = tokens.shape
    n, f = routed.shape[1], w_up.shape[1]
    batch = lax.axis_size("batch")
    s = Sizes(rows, d, n, f, batch)
    found = scratch_of(s)
    vmem, smem, anywhere = (pl.BlockSpec(memory_space=space) for space in (pltpu.VMEM, pltpu.SMEM, pl.ANY))
    shape = pltpu.VMEM if s.folds else jax.ShapeDtypeStruct
    block_out, att, vec, grad_tokens, mlp = pl.pallas_call(
        functools.partial(layer_kernel, s, tuple(found)),
        out_shape=(
            shape(tokens.shape, LOW),
            shape((4, s.pairs, s.block, s.pair), LOW) if s.folds else shape((s.pairs, d, s.pair), F32),
            shape((8, s.block if s.folds else d), F32),
            jax.ShapeDtypeStruct(tokens.shape, LOW),
            jax.ShapeDtypeStruct((2, *s.tail, f), F32),
        ),
        in_specs=[anywhere] * 3 + [smem] + [anywhere] * 8,
        out_specs=[vmem] * 3 + [anywhere] * 2,
        scratch_shapes=list(found.values()),
        compiler_params=pltpu.CompilerParams(collective_id=0, has_side_effects=True, vmem_limit_bytes=VMEM_BYTES),
        name="layer",
    )(
        tokens, cotangent, key_mask, lengths, routed, w_router, gain_one, gain_two, w_qkv, w_out, w_up, w_down,
    )
    if s.folds:
        block_out, grad_tokens, g_up, g_down, g_qkv, g_out, *g_vecs = hand_over(block_out, att, vec, grad_tokens, mlp)
    else:
        mlp = lax.psum_scatter(mlp, "batch", scatter_dimension=1, tiled=True)
        vec = lax.psum_scatter(vec, "batch", scatter_dimension=1, tiled=True)
        att = lax.psum_scatter(att, "batch", scatter_dimension=1, tiled=True).astype(LOW)
        att = lax.all_gather(att, "mp", axis=0).astype(F32)
        att = jnp.transpose(att, (2, 0, 1, 3)).reshape(s.block, 4 * d)
        (g_up, g_down), g_qkv, g_out, g_vecs = mlp, att[:, : 3 * d], att[:, 3 * d :], vec[:3]
    g_router, g_one, g_two = (g.reshape(s.block) for g in g_vecs)
    return block_out, grad_tokens, g_router, g_one, g_two, g_qkv, g_out, g_up, g_down.T


def solution(mesh):
    rows_spec = P(("batch", "mp"), None, None)
    in_specs = (
        rows_spec,
        P(("batch", "mp"), None),
        P(("batch", "mp")),
        P(("batch", "mp"), None),
        P(),
        P(),
        P(),
        P(),
        P(),
        P(None, "mp"),
        P("mp", None),
        rows_spec,
    )
    out_specs = (
        rows_spec,
        rows_spec,
        P("batch"),
        P("batch"),
        P("batch"),
        P("batch", None),
        P("batch", None),
        P("batch", "mp"),
        P("mp", "batch"),
    )
    return jax.shard_map(local, mesh=mesh, in_specs=in_specs, out_specs=out_specs, check_vma=False)
```

time: 90.4 us -> 87.3 us (0.966)
  Pallas kernels: 88.7 us -> 85.7 us
    pallas_call x1, Pallas kernels: 83.3 us -> 80.1 us  [local(): pl.pallas_call(functools.partial(layer_kernel, s, tuple(found)), out_shap...]
where the time goes in v3:
time: 87.3 us; the launch traced here: 87.2 us
  Pallas kernels  85.7 us (98%)
  between operations  1.48 us (2%)
    pallas_call x1, Pallas kernels, local(): pl.pallas_call(functools.partial(layer_kernel, s, tuple(found)), out_shap...  80.1 us
    pallas_call x1, Pallas kernels, hand_over(): pl.pallas_call(hand_over_kernel, out_shape=[*[jax.ShapeDtypeStruct(block_...  5.62 us

profile of v3, /device:TPU:0, one launch (start us, length us, event | category | flops | bytes accessed | tf_op | source)
XLA Modules:
  0.0 87.2 jit_solution(18156683525366554967)
XLA Ops:
  1.3 80.1 %layer.1 = (bf16[1,2048,768]{2,1,0:T(8,128)(2,1)S(1)}, bf16[4,6,96,128]{3,2,1,0:T(8,128)(2,1)S(1)}, f32[8,96]{1,0:T(8,128)S(1)}, bf16[1,2048,768]{2,1,0:T(8,128)(2,1)}, f32[2,96,768]{2,1,0:T(8,128)}) custom-call(bf16[1,2048,768]{2,1,0:T(8,128)(2,1)} %refs_0_.1, bf16[1,2048,768]{2,1,0:T(8,128)(2,1)} %refs_1_.1, s32[1,2048]{1,0:T(1,128)} %refs_2_.1, ...), custom_call_target="tpu_custom_call" | custom-call | tf_op jit(solution)/shard_map/layer/pallas_call | solution.py:697
  81.4 5.6 %hand_over.1 = (bf16[1,2048,768]{2,1,0:T(8,128)(2,1)}, bf16[1,2048,768]{2,1,0:T(8,128)(2,1)}, f32[96,768]{1,0:T(8,128)}, f32[96,768]{1,0:T(8,128)}, f32[96,2304]...) custom-call(bf16[1,2048,768]{2,1,0:T(8,128)(2,1)S(1)} %get-tuple-element.23.block_out, ...), custom_call_target="tpu_custom_call" | custom-call | tf_op jit(solution)/shard_map/hand_over/pallas_call | solution.py:668

commit v4 on v3

--- a/solution.py
+++ b/solution.py
@@ -16,15 +16,15 @@
 MESH = pl.DeviceIdType.MESH
 VMEM_BYTES = 58 * 2**20
 AXES = "dxbay"
-MLP_ORDERS = ("yab", "aby", "yab", "yab", "aby", "yab")
-ATT_ORDERS = ("dxyab", "dxyab", "dxaby", "dyxabG", "dxyabG", "daxyb")
+MLP_ORDERS = ("yab", "aby", "yab", "aby", "yab", "yab")
+ATT_ORDERS = ("dxyabG", "dxyabG", "dxaybG", "daxybG", "dyxab", "dxyabG")
 SEQUENCE = (
-    ("f0", "f1", "u0", "u1", "u2", "u3", "u4", "u5", "w0", "w1", "w2", "w3", "w4", "t", "r0", "r1", "w5"),
-    ("r2", "r3", "b0", "m1", "b1", "m0", "a0", "b2", "a1", "b3", "m4", "a2", "m2", "b4", "a3", "o0", "b5"),
-    ("a4", "m0", "e0", "m1", "a5", "a0", "m3", "e1", "m2", "m4", "m5", "a1", "m0", "a3", "a5", "a2", "o1"),
-    ("m3", "z", "m1", "s0", "s1", "a4", "v", "m2", "a0", "m5", "s2", "s3", "m4", "a3", "s4", "s5", "a2", "s6"),
-    ("s7", "a5", "a1", "v", "a0", "m3", "a4", "a3", "m5", "a5", "v", "a1", "a2", "a4", "a0", "a3", "v", "a5"),
-    ("a2", "a1", "a0", "a4", "a0", "a3", "a5", "a2", "v", "a1", "a5", "a2", "a1", "a4"),
+    ("f0", "f1", "u1", "u0", "t", "w1", "u4", "u5", "w0", "u3", "w5", "r0", "r1", "w3", "r3", "u2", "r2"),
+    ("b0", "w2", "m1", "w4", "a0", "b3", "m0", "b1", "m3", "b2", "a1", "a3", "b4", "b5", "o0", "m2", "m5"),
+    ("a4", "a2", "a0", "a5", "m4", "m0", "o1", "a1", "e0", "a2", "e1", "a3", "z", "m3", "s6", "m2", "a4"),
+    ("v", "a0", "a5", "s4", "m4", "a1", "m5", "a3", "a2", "s3", "a4", "a0", "v", "a5", "a3", "a1", "m1", "a4"),
+    ("v", "a2", "m5", "a5", "a0", "s1", "a3", "m3", "a1", "s0", "v", "a4", "a2", "s7", "s5", "a5", "m1", "m0"),
+    ("m2", "a0", "s2", "m4", "a1", "a4", "a3", "v", "a2", "a4", "a5"),
 )
 
 
@@ -110,6 +110,7 @@
         mask_row=pltpu.VMEM((1, s.rows), jnp.int32),
         wanted_row=pltpu.VMEM((1, n), jnp.int32),
         gres=pltpu.VMEM((n, d), F32),
+        gfirst=pltpu.VMEM((n, d), F32),
         gatt=pltpu.VMEM((n, d), LOW),
         gmix=pltpu.VMEM((n, d), LOW),
         dqkv=pltpu.VMEM((n, 3 * d), LOW),
@@ -376,12 +377,12 @@
         cols = slice(at % 3 * s.part, (at % 3 + 1) * s.part)
         return mm(left[...], right[w, :, cols])
 
-    sent_core = []
+    sent_core = {}
 
     def other_core(at):
         table = getattr(v, f"u{at}")
         table[...] = weight_grad(at, 1).astype(LOW).reshape(table.shape)
-        sent_core.append(send(table, getattr(v, f"m{at}_0"), "d"))
+        sent_core[at] = send(table, getattr(v, f"m{at}_0"), "d")
 
     class Sum:
         def __init__(self, name, axes, order, finish):
@@ -544,13 +545,14 @@
     kept = {}
 
     def first_back(at):
-        rows = slice(at * half, (at + 1) * half)
-        gfirst = mm(v.dqkv[rows], v.wqkv[...], 1, 1)
-        picked, rate = v.picked[rows], rate_one[rows]
-        kept[at] = jnp.sum(gfirst * (picked * rate), axis=0, keepdims=True)
+        if at == 0:
+            v.gfirst[...] = mm(v.dqkv[...], v.wqkv[...], 1, 1)
+            return
+        gfirst, picked, rate = v.gfirst[...], v.picked[...], rate_one
+        kept["gain_one"] = jnp.sum(gfirst * (picked * rate), axis=0, keepdims=True)
         scaled = gfirst * one_row
         gnorm = rate * scaled - picked * (rate * rate * rate * jnp.mean(scaled * picked, axis=1, keepdims=True))
-        v.gres[rows] = v.gres[rows] + gnorm
+        v.gres[...] = v.gres[...] + gnorm
 
     def finish_rows():
         picked = v.picked[...]
@@ -562,7 +564,7 @@
         v.upd_tok[...] = (live * (v.gres[...] + glogit * router_row)).astype(LOW)
         row = iota((8, d), 0)
         gain_two_sum = sum(gain_two_sums)
-        v.vec[0] = jnp.where(row == 0, router_sum, jnp.where(row == 1, kept[0] + kept[1], jnp.where(row == 2, gain_two_sum, 0.0)))
+        v.vec[0] = jnp.where(row == 0, router_sum, jnp.where(row == 1, kept["gain_one"], jnp.where(row == 2, gain_two_sum, 0.0)))
         sums["v"] = Everywhere("dxyab" if s.folds else "dx")
 
     tile = s.rows // 8

time: 87.3 us -> 86 us (0.985)
  Pallas kernels: 85.7 us -> 84.4 us
    pallas_call x1, Pallas kernels: 80.1 us -> 78.8 us  [local(): pl.pallas_call(functools.partial(layer_kernel, s, tuple(found)), out_shap...]
where the time goes in v4:
time: 86 us; the launch traced here: 85.9 us
  Pallas kernels  84.4 us (98%)
  between operations  1.48 us (2%)
    pallas_call x1, Pallas kernels, local(): pl.pallas_call(functools.partial(layer_kernel, s, tuple(found)), out_shap...  78.8 us
    pallas_call x1, Pallas kernels, hand_over(): pl.pallas_call(hand_over_kernel, out_shape=[*[jax.ShapeDtypeStruct(block_...  5.62 us

profile of v4, /device:TPU:0, one launch (start us, length us, event | category | flops | bytes accessed | tf_op | source)
XLA Modules:
  0.0 85.9 jit_solution(10518458904813121290)
XLA Ops:
  1.3 78.8 %layer.1 = (bf16[1,2048,768]{2,1,0:T(8,128)(2,1)S(1)}, bf16[4,6,96,128]{3,2,1,0:T(8,128)(2,1)S(1)}, f32[8,96]{1,0:T(8,128)S(1)}, bf16[1,2048,768]{2,1,0:T(8,128)(2,1)}, f32[2,96,768]{2,1,0:T(8,128)}) custom-call(bf16[1,2048,768]{2,1,0:T(8,128)(2,1)} %refs_0_.1, bf16[1,2048,768]{2,1,0:T(8,128)(2,1)} %refs_1_.1, s32[1,2048]{1,0:T(1,128)} %refs_2_.1, ...), custom_call_target="tpu_custom_call" | custom-call | tf_op jit(solution)/shard_map/layer/pallas_call | solution.py:699
  80.1 5.6 %hand_over.1 = (bf16[1,2048,768]{2,1,0:T(8,128)(2,1)}, bf16[1,2048,768]{2,1,0:T(8,128)(2,1)}, f32[96,768]{1,0:T(8,128)}, f32[96,768]{1,0:T(8,128)}, f32[96,2304]...) custom-call(bf16[1,2048,768]{2,1,0:T(8,128)(2,1)S(1)} %get-tuple-element.23.block_out, ...), custom_call_target="tpu_custom_call" | custom-call | tf_op jit(solution)/shard_map/hand_over/pallas_call | solution.py:670

commit v5 on v4

--- a/solution.py
+++ b/solution.py
@@ -512,6 +512,8 @@
             spilt["mo"].wait_recv()
             v.mo[work:n] = v.spill_in[3].astype(F32)
 
+    out_made = []
+
     def attend_back(p):
         where = [slice(g * d + p * pair, g * d + (p + 1) * pair) for g in range(3)]
         q, k, val = (v.qkv[:, cols] for cols in where)
@@ -538,7 +540,12 @@
         table[0, 0] = both[:, :pair].reshape(shape)
         table[1, 0] = both[:, pair:].reshape(shape)
         table[0, 1] = mm(v.first_t[...], lower[2]).astype(LOW).reshape(shape)
-        table[1, 1] = mm(v.mixed_t[...], v.gatt[:, p * pair : (p + 1) * pair]).astype(LOW).reshape(shape)
+        two = p - p % 2
+        if two not in out_made:
+            out_made.append(two)
+            wide = mm(v.mixed_t[...], v.gatt[:, two * pair : (two + 2) * pair]).astype(LOW)
+            getattr(v, f"a{two}_0")[1, 1] = wide[:, :pair].reshape(shape)
+            getattr(v, f"a{two + 1}_0")[1, 1] = wide[:, pair:].reshape(shape)
         order = s.att_orders[p]
         sums[f"a{p}"] = Sum(f"a{p}", "dxbay" if s.folds else "dx", order.strip("G"), Gather(p, "G" in order))
 
@@ -623,7 +630,7 @@
 
 
 def hand_over_kernel(block_out, att, vec, grad_tokens, mlp, out, tok, g_up, g_down, g_qkv, g_out, *rest):
-    *vecs, tok_buf, mlp_buf, qkv_buf, out_buf, come_sem, go_sem = rest
+    vecs, (tok_buf, mlp_buf, qkv_buf, out_buf, *vec_bufs, come_sem, go_sem) = rest[:3], rest[3:]
     _, pairs, _, pair = att.shape
     d = g_out.shape[1]
     rows = tok.shape[1] // 4
@@ -647,8 +654,9 @@
         out_buf[:, p * pair : (p + 1) * pair] = att[3, p].astype(F32)
     go(qkv_buf, g_qkv)
     go(out_buf, g_out)
-    for at, row in enumerate(vecs):
-        row[...] = vec[at : at + 1]
+    for at in range(3):
+        vec_bufs[at][...] = vec[at : at + 1]
+        go(vec_bufs[at], vecs[at])
     for at in range(4):
         coming[at].wait()
         there = pl.ds(at * rows, rows)
@@ -675,13 +683,14 @@
             *[jax.ShapeDtypeStruct((1, block), F32)] * 3,
         ],
         in_specs=[vmem] * 3 + [hbm] * 2,
-        out_specs=[anywhere] * 6 + [vmem] * 3,
+        out_specs=[anywhere] * 9,
         scratch_shapes=[
             pltpu.VMEM((rows, d), LOW),
             pltpu.VMEM(mlp.shape, F32),
             *[pltpu.VMEM(shape, dtype) for shape, dtype in shapes[2:]],
+            *[pltpu.VMEM((1, block), F32)] * 3,
             pltpu.SemaphoreType.DMA((6,)),
-            pltpu.SemaphoreType.DMA((9,)),
+            pltpu.SemaphoreType.DMA((12,)),
         ],
         compiler_params=pltpu.CompilerParams(vmem_limit_bytes=16 * 2**20),
         name="hand_over",

time: 86 us -> 85.5 us (level)
  no operation moved by 1% of the time
where the time goes in v5:
time: 85.5 us; the launch traced here: 85.4 us
  Pallas kernels  83.9 us (98%)
  between operations  1.48 us (2%)
    pallas_call x1, Pallas kernels, local(): pl.pallas_call(functools.partial(layer_kernel, s, tuple(found)), out_shap...  78.8 us
    pallas_call x1, Pallas kernels, hand_over(): pl.pallas_call(hand_over_kernel, out_shape=[*[jax.ShapeDtypeStruct(block_...  5.13 us

profile of v5, /device:TPU:0, one launch (start us, length us, event | category | flops | bytes accessed | tf_op | source)
XLA Modules:
  0.0 85.4 jit_solution(3107884183345000823)
XLA Ops:
  1.3 78.8 %layer.1 = (bf16[1,2048,768]{2,1,0:T(8,128)(2,1)S(1)}, bf16[4,6,96,128]{3,2,1,0:T(8,128)(2,1)S(1)}, f32[8,96]{1,0:T(8,128)S(1)}, bf16[1,2048,768]{2,1,0:T(8,128)(2,1)}, f32[2,96,768]{2,1,0:T(8,128)}) custom-call(bf16[1,2048,768]{2,1,0:T(8,128)(2,1)} %refs_0_.1, bf16[1,2048,768]{2,1,0:T(8,128)(2,1)} %refs_1_.1, s32[1,2048]{1,0:T(1,128)} %refs_2_.1, ...), custom_call_target="tpu_custom_call" | custom-call | tf_op jit(solution)/shard_map/layer/pallas_call | solution.py:708
  80.1 5.1 %hand_over.1 = (bf16[1,2048,768]{2,1,0:T(8,128)(2,1)}, bf16[1,2048,768]{2,1,0:T(8,128)(2,1)}, f32[96,768]{1,0:T(8,128)}, f32[96,768]{1,0:T(8,128)}, f32[96,2304]...) custom-call(bf16[1,2048,768]{2,1,0:T(8,128)(2,1)S(1)} %get-tuple-element.23.block_out, ...), custom_call_target="tpu_custom_call" | custom-call | tf_op jit(solution)/shard_map/hand_over/pallas_call | solution.py:678
